TPU v7x, 256 devices: a whole 4x4x8 slice. The times are simulated.
256 devices in a mesh: segment: 4 (over x_hi, core), space: 64 (over z, y, x_lo).
Axes of the slice: x: 4 (x_hi: 2, x_lo: 2; x = x_hi * 2 + x_lo), y: 4, z: 8, core: 2. Of those that a mesh axis runs over, the one named last changes fastest.
Arguments:
- clean_frames: float32 [2, 4096, 64], P(None, 'space'), may hold values from -6 to 6
- noise: float32 [2, 4096, 64], P(None, 'space'), may hold values from -6 to 6
- noise_steps: int32 [2], replicated, may hold values from 0 to 999
- noise_freqs: float32 [128], replicated, may hold values from -4 to 4
- cond_weights: bfloat16 [4, 256, 1024], P('segment'), may hold values from -0.375 to 0.375
- patch_in: float32 [16, 1024], replicated, may hold values from -1.5 to 1.5
- patch_out: bfloat16 [1024, 16], replicated, may hold values from -0.1875 to 0.1875
- section_weights: bfloat16 [4, 6144, 1024], P('segment'), may hold values from -0.1875 to 0.1875
- head_scales: float32 [4, 24], P('segment'), may hold values from 1.5 to 10
- fine_links: int32 [128, 2, 9], P('space'), may hold values from 0 to 1, as said below
- coarse_links: int32 [64, 1, 9], P('space'), may hold values from 0 to 1, as said below
Outputs:
- prediction: float32 [2, 4096, 64], P(None, 'space', 'segment')
Inputs may be any that keep to these rules, and one draw needn't show every extreme that they name: `fine_links`: entry 3 (dy + 1) + (dx + 1) is 1 where the tile attends to the tile dy tile rows down and dx tile columns right: always for the tile itself, never for a tile outside the grid. `coarse_links`: entry 3 (dy + 1) + (dx + 1) is 1 where the tile attends to the tile dy tile rows down and dx tile columns right: always for the tile itself, never for a tile outside the grid.
All inputs are finite; a program needn't handle non-finite values.
Results may differ from a plain program's by a relative error of at most 0.019.
Values may be sent and summed in bfloat16 or wider, within the bound.
A program may use at most 192 MiB of HBM per device.

v0:
```python
import math

import jax
import jax.numpy as jnp
from jax import lax
from jax.sharding import PartitionSpec as P

HS = 64
H0 = 8
STEPS = 1000
MB = 2


LOG_LOW = math.log(0.002)
LOG_HIGH = math.log(80.0)


def shortened(shard):
    return jax.tree.map(lambda a: a.astype(jnp.bfloat16) if a.dtype == jnp.float32 else a, shard)


def padded_2(shard, sides, width):
    for axis, dim in sides:
        count, length = (lax.axis_size(axis), shard.shape[dim])
        up = [(i, (i + 1) % count) for i in range(count - 1)]
        down = [(j, i) for i, j in up]
        last = lax.slice_in_dim(shard, length - width, length, axis=dim)
        leading = lax.slice_in_dim(shard, 0, width, axis=dim)
        before = lax.ppermute(last, axis, up)
        after = lax.ppermute(leading, axis, down)
        shard = jnp.concatenate([before, shard, after], axis=dim)
    return shard


def shifted(block, axis, distance):
    devices = range(lax.axis_size(axis))
    route = [(i - distance, i) for i in devices if i - distance in devices]
    return lax.ppermute(block, axis, route)


def broadcast(value, axis, source):
    kept = jnp.where(lax.axis_index(axis) == source, value, 0).astype(value.dtype)
    return lax.psum(kept, axis)


def window_tables():
    query_row = jnp.arange(64) // 8
    query_col = jnp.arange(64) % 8
    key_row = jnp.arange(196) // 14
    key_col = jnp.arange(196) % 14
    inside = (jnp.abs(key_row[None, :] - 3 - query_row[:, None]) <= 3) & (
        jnp.abs(key_col[None, :] - 3 - query_col[:, None]) <= 3
    )
    row_step = (key_row >= 3).astype(jnp.int32) + (key_row >= 11).astype(jnp.int32)
    col_step = (key_col >= 3).astype(jnp.int32) + (key_col >= 11).astype(jnp.int32)
    pickers = (jnp.arange(9)[:, None] == (3 * row_step + col_step)[None, :]).astype(jnp.float32)
    return (inside.astype(jnp.float32), pickers)


def rms_rows(stream):
    return stream * lax.rsqrt(jnp.mean(stream * stream, axis=-1, keepdims=True) + 1e-06)


def unit_heads(values, head_width):
    shaped = values.reshape(values.shape[:-1] + (values.shape[-1] // head_width, head_width))
    return rms_rows(shaped).reshape(values.shape)


def times_stored(left_rows, stored):
    return lax.dot_general(
        left_rows, stored, (((1,), (1,)), ((), ())), preferred_element_type=jnp.float32
    )


def project_all(normed, w_qkv, inner_width):
    row_count, col_count = (normed.shape[0], normed.shape[1])
    projected = times_stored(normed.reshape(row_count * col_count, -1), w_qkv)
    projected = projected.reshape(row_count, col_count, 3 * inner_width)
    queries = unit_heads(projected[..., :inner_width], HS).astype(jnp.bfloat16)
    key_part = unit_heads(projected[..., inner_width : 2 * inner_width], HS).astype(jnp.bfloat16)
    value_part = projected[..., 2 * inner_width :].astype(jnp.bfloat16)
    return (queries, jnp.concatenate([key_part, value_part], axis=-1))


def local_attention(queries, extended_kv, tile_links, scales):
    row_count, col_count, inner_width = queries.shape
    head_count = scales.shape[0]
    head_width = inner_width // head_count
    tile_rows = row_count // 8
    tile_cols = col_count // 8
    padded = jnp.pad(extended_kv, ((0, 0), (3, 3), (0, 0)))
    key_bands = jnp.stack(
        [
            jnp.stack(
                [
                    padded[8 * tile_row : 8 * tile_row + 14, 8 * tile_col : 8 * tile_col + 14]
                    for tile_col in range(tile_cols)
                ],
                0,
            )
            for tile_row in range(tile_rows)
        ],
        0,
    )
    key_bands = key_bands.reshape(tile_rows, tile_cols, 196, 2 * inner_width)
    key_part = key_bands[..., :inner_width].reshape(
        tile_rows, tile_cols, 196, head_count, head_width
    )
    value_part = key_bands[..., inner_width:].reshape(
        tile_rows, tile_cols, 196, head_count, head_width
    )
    query_tiles = queries.reshape(tile_rows, 8, tile_cols, 8, head_count, head_width).transpose(
        0, 2, 1, 3, 4, 5
    )
    query_tiles = query_tiles.reshape(tile_rows, tile_cols, 64, head_count, head_width)
    window, pickers = window_tables()
    allowed = (
        window[None, None]
        * jnp.einsum("tcn,nk->tck", tile_links.astype(jnp.float32), pickers)[:, :, None, :]
    )
    scores = jnp.einsum(
        "tcqhd,tckhd->tchqk", query_tiles, key_part, preferred_element_type=jnp.float32
    )
    expo = jnp.exp(scores * (scales / head_width)[:, None, None]) * allowed[:, :, None]
    weighting = (expo / jnp.sum(expo, axis=-1, keepdims=True)).astype(jnp.bfloat16)
    mixture = jnp.einsum(
        "tchqk,tckhd->tcqhd", weighting, value_part, preferred_element_type=jnp.float32
    ).astype(jnp.bfloat16)
    mixture = mixture.reshape(tile_rows, tile_cols, 8, 8, inner_width).transpose(0, 2, 1, 3, 4)
    return mixture.reshape(row_count, col_count, inner_width)


def per_device(
    clean_frames,
    noise,
    noise_steps,
    noise_freqs,
    cond_weights,
    patch_in,
    patch_out,
    section_weights,
    head_scales,
    fine_links,
    coarse_links,
):
    segment_index = lax.axis_index("segment")
    weights = section_weights[0]
    scales = head_scales[0]
    model_width = weights.shape[1]
    fine_rows = clean_frames.shape[1] // 4
    fine_cols = clean_frames.shape[2] // 4
    coarse_rows = fine_rows // 2
    coarse_cols = fine_cols // 2
    fine_inner = H0 * HS
    coarse_inner = weights.shape[0] // 4
    fine_qkv = weights[: 3 * fine_inner]
    fine_out = weights[3 * fine_inner : 4 * fine_inner]
    resize_rows = weights[4 * fine_inner :]
    coarse_qkv = weights[: 3 * coarse_inner]
    coarse_out = weights[3 * coarse_inner :]
    fine_scales = scales[:H0]
    lanes = fine_cols * coarse_inner
    noise_level = jnp.exp(
        LOG_LOW + noise_steps.astype(jnp.float32) / (STEPS - 1) * (LOG_HIGH - LOG_LOW)
    )
    phases = 2.0 * math.pi * (jnp.log(noise_level) / 4.0)[:, None] * noise_freqs[None, :]
    features = jnp.concatenate([jnp.cos(phases), jnp.sin(phases)], axis=1)
    gains = 1.0 + jnp.dot(
        features, cond_weights[0].astype(jnp.float32), precision=lax.Precision.HIGHEST
    )

    def embed(micro_index):
        frame = lax.dynamic_index_in_dim(clean_frames, micro_index, 0, keepdims=False)
        fresh = lax.dynamic_index_in_dim(noise, micro_index, 0, keepdims=False)
        level = lax.dynamic_index_in_dim(noise_level, micro_index, 0, keepdims=False)
        scaled = (frame + level * fresh) * lax.rsqrt(level * level + 0.25)
        patches = (
            scaled.reshape(fine_rows, 4, fine_cols, 4)
            .transpose(0, 2, 1, 3)
            .reshape(fine_rows * fine_cols, 16)
        )
        embedded = jnp.dot(
            patches, patch_in, precision=lax.Precision.HIGHEST, preferred_element_type=jnp.float32
        )
        return embedded.reshape(fine_rows, fine_cols, model_width)

    def fine_zero():
        return (
            jnp.zeros((fine_rows, fine_cols, model_width), jnp.float32),
            jnp.zeros((fine_rows, fine_cols, model_width), jnp.bfloat16),
            jnp.zeros((fine_rows, fine_cols, fine_inner), jnp.bfloat16),
            jnp.zeros((fine_rows, fine_cols, 2 * fine_inner), jnp.bfloat16),
        )

    def coarse_zero():
        return (
            jnp.zeros((coarse_rows, coarse_cols, model_width), jnp.float32),
            jnp.zeros((coarse_rows, coarse_cols, model_width), jnp.bfloat16),
            jnp.zeros((coarse_rows, coarse_cols, coarse_inner), jnp.bfloat16),
            jnp.zeros((coarse_rows, coarse_cols, 2 * coarse_inner), jnp.bfloat16),
        )

    def make_edges(kv_block):
        outer = jnp.concatenate([kv_block[:3], kv_block[-3:]], axis=0).reshape(6, -1)
        return jnp.pad(outer, ((0, 0), (0, lanes - outer.shape[1])))

    def neighbour_kv(extended, col_count, inner_width):
        outer = jnp.concatenate([extended[:3], extended[9:]], axis=0)
        found = outer[:, : col_count * 2 * inner_width].reshape(6, col_count, 2 * inner_width)
        return (found[:3], found[3:])

    def merge_tokens(skip_fine):
        grouped = skip_fine.reshape(coarse_rows, 2, coarse_cols, 2, model_width).transpose(
            0, 2, 1, 3, 4
        )
        grouped = grouped.reshape(coarse_rows * coarse_cols, 4 * model_width)
        merged = jnp.dot(grouped, resize_rows, preferred_element_type=jnp.float32).astype(
            jnp.bfloat16
        )
        return merged.reshape(coarse_rows, coarse_cols, model_width)

    def split_tokens(coarse_in):
        widened = times_stored(
            coarse_in.reshape(coarse_rows * coarse_cols, model_width), resize_rows
        )
        widened = widened.reshape(coarse_rows, coarse_cols, 2, 2, model_width).transpose(
            0, 2, 1, 3, 4
        )
        return widened.reshape(fine_rows, fine_cols, model_width)

    def pixel_head(fine_up):
        normed_top = rms_rows(fine_up).astype(jnp.bfloat16)
        pixels = jnp.dot(
            normed_top.reshape(fine_rows * fine_cols, model_width),
            patch_out,
            preferred_element_type=jnp.float32,
        )
        return (
            pixels.reshape(fine_rows, fine_cols, 4, 4)
            .transpose(0, 2, 1, 3)
            .reshape(4 * fine_rows, 4 * fine_cols)
        )

    inbound = jnp.zeros((coarse_rows, coarse_cols, model_width), jnp.bfloat16)
    skip_store = jnp.zeros((MB, fine_rows, fine_cols, model_width), jnp.bfloat16)
    predicted = jnp.zeros((MB, 4 * fine_rows, 4 * fine_cols), jnp.float32)
    branch_base = (
        1 + (segment_index >= 1).astype(jnp.int32) + (segment_index >= 3).astype(jnp.int32)
    )
    for moment in range(MB + 3):
        micro_index = moment - segment_index
        active = (micro_index >= 0) & (micro_index < MB)
        clamped = jnp.clip(micro_index, 0, MB - 1)
        gain_row = lax.dynamic_index_in_dim(gains, clamped, 0, keepdims=False)
        skip_now = lax.dynamic_index_in_dim(skip_store, clamped, 0, keepdims=False)
        selector = jnp.where(active, branch_base, 0)

        def fine_front(stream):
            normed = (rms_rows(stream) * gain_row).astype(jnp.bfloat16)
            queries, kv_block = project_all(normed, fine_qkv, fine_inner)
            return ((stream, normed, queries, kv_block), coarse_zero(), make_edges(kv_block))

        def spare_front():
            return (fine_zero(), coarse_zero(), jnp.zeros((6, lanes), jnp.bfloat16))

        def first_front():
            return fine_front(embed(clamped))

        def middle_front():
            stream = inbound.astype(jnp.float32)
            normed = (rms_rows(stream) * gain_row).astype(jnp.bfloat16)
            queries, kv_block = project_all(normed, coarse_qkv, coarse_inner)
            return (fine_zero(), (stream, normed, queries, kv_block), make_edges(kv_block))

        def last_front():
            return fine_front(split_tokens(inbound) + skip_now.astype(jnp.float32))

        fine_state, coarse_state, edges = lax.switch(
            selector, [spare_front, first_front, middle_front, last_front]
        )
        extended = padded_2(shortened(edges), (("space", 0),), 3).astype(edges.dtype)

        def fine_block():
            stream, normed, queries, kv_block = fine_state
            rows_above, rows_below = neighbour_kv(extended, fine_cols, fine_inner)
            full_kv = jnp.concatenate([rows_above, kv_block, rows_below], axis=0)
            mixture = local_attention(queries, full_kv, fine_links, fine_scales)
            update = jnp.dot(
                mixture.reshape(fine_rows * fine_cols, fine_inner),
                fine_out,
                preferred_element_type=jnp.float32,
            )
            return stream + update.reshape(fine_rows, fine_cols, model_width)

        def spare_back():
            return (
                jnp.zeros((coarse_rows, coarse_cols, model_width), jnp.bfloat16),
                jnp.zeros((fine_rows, fine_cols, model_width), jnp.bfloat16),
                jnp.zeros((4 * fine_rows, 4 * fine_cols), jnp.float32),
            )

        def first_back():
            skip_fine = fine_block().astype(jnp.bfloat16)
            return (
                merge_tokens(skip_fine),
                skip_fine,
                jnp.zeros((4 * fine_rows, 4 * fine_cols), jnp.float32),
            )

        def middle_back():
            stream, normed, queries, kv_block = coarse_state
            rows_above, rows_below = neighbour_kv(extended, coarse_cols, coarse_inner)
            full_kv = jnp.concatenate([rows_above, kv_block, rows_below], axis=0)
            mixture = local_attention(queries, full_kv, coarse_links, scales)
            update = jnp.dot(
                mixture.reshape(coarse_rows * coarse_cols, coarse_inner),
                coarse_out,
                preferred_element_type=jnp.float32,
            )
            result = stream + update.reshape(coarse_rows, coarse_cols, model_width)
            return (
                result.astype(jnp.bfloat16),
                jnp.zeros((fine_rows, fine_cols, model_width), jnp.bfloat16),
                jnp.zeros((4 * fine_rows, 4 * fine_cols), jnp.float32),
            )

        def last_back():
            pixels = pixel_head(fine_block())
            return (
                jnp.zeros((coarse_rows, coarse_cols, model_width), jnp.bfloat16),
                jnp.zeros((fine_rows, fine_cols, model_width), jnp.bfloat16),
                pixels,
            )

        outbound, skip_out, pixels = lax.switch(
            selector, [spare_back, first_back, middle_back, last_back]
        )
        landing = (jnp.arange(MB) == micro_index)[:, None, None] & (segment_index == 3)
        predicted = jnp.where(landing, pixels[None], predicted)
        if moment < MB + 2:
            inbound = jax.tree.map(
                lambda part, own: part.astype(own.dtype),
                shifted(shortened(outbound), "segment", 1),
                outbound,
            )
            if moment < MB:
                arrived = jax.tree.map(
                    lambda part, own: part.astype(own.dtype),
                    shifted(shortened(skip_out), "segment", 3),
                    skip_out,
                )
                skip_store = skip_store.at[moment].set(arrived)
    everywhere = broadcast(shortened(predicted), "segment", 3).astype(predicted.dtype)
    return lax.dynamic_slice_in_dim(everywhere, segment_index * fine_cols, fine_cols, 2)


def solution(mesh):
    in_specs = (
        P(None, "space", None),
        P(None, "space", None),
        P(),
        P(),
        P("segment", None, None),
        P(),
        P(),
        P("segment", None, None),
        P("segment", None),
        P("space", None, None),
        P("space", None, None),
    )
    out_specs = P(None, "space", "segment")
    return jax.shard_map(
        per_device, mesh=mesh, in_specs=in_specs, out_specs=out_specs, check_vma=False
    )
```

profile of v0, /device:TPU:122, one launch (start us, length us, event | category | flops | bytes accessed | tf_op | source)
XLA Modules:
  0.0 405.4 jit_solution(6735430195368821428)
XLA Ops:
  0.0 6.4 %slice_bitcast_fusion.2 = (bf16[1536,1024]{1,0:T(8,128)(2,1)}, bf16[1536,1024]{1,0:T(8,128)(2,1)}) fusion(bf16[1,6144,1024]{2,1,0:T(8,128)(2,1)} %param.62), kind=kLoop, calls=%fused_computation.1128 | loop fusion | bytes 12582912 | tf_op jit(solution)/shard_map/slice | solution.py:160
  6.4 7.7 %slice_bitcast_fusion.1 = bf16[4096,1024]{1,0:T(8,128)(2,1)} fusion(bf16[1,6144,1024]{2,1,0:T(8,128)(2,1)} %param.62), kind=kLoop, calls=%fused_computation.1127 | loop fusion | bytes 16777216 | tf_op jit(solution)/shard_map/slice | solution.py:158
  14.1 8.6 %slice_bitcast_fusion = bf16[4608,1024]{1,0:T(8,128)(2,1)} fusion(bf16[1,6144,1024]{2,1,0:T(8,128)(2,1)} %param.62), kind=kLoop, calls=%fused_computation.1126 | loop fusion | bytes 18874368 | tf_op jit(solution)/shard_map/slice | solution.py:159
  24.3 25.2 %conditional.10 = (f32[16,16,1024]{2,1,0:T(8,128)}, bf16[16,16,512]{2,1,0:T(8,128)(2,1)S(1)}, bf16[16,16,1024]{2,1,0:T(8,128)(2,1)S(1)}, bf16[8,8,1536]{2,1,0:T(...) conditional(s32[]{:T(128)} %clamp.24, () %tuple.205, ...), branch_computations={%region_0.1_spmd, %region_1.5_spmd, %region_5.8_spmd, %region_8.12... | conditional | flops 1346081024 | bytes 53522616 | solution.py:278
  51.0 4.7 %collective-permute-start = (bf16[3,24576]{1,0:T(4,128)(2,1)S(1)}, bf16[3,24576]{1,0:T(4,128)(2,1)S(1)}, u32[]{:S(2)}, u32[]{:S(2)}) collective-permute-start(bf16[3,24576]{1,0:T(4,128)(2,1)S(1)} %get-tuple-element.1201), channel_id=1, source_target_pairs={{0,1},{1,2},{2,3},{3,4},{4,5},{5,6},{6,7},{7,8},{8,9},{9,10},{10,1... | collective-permute-start | bytes 442376 | tf_op jit(solution)/shard_map/ppermute | solution.py:29
  59.5 8.0 %collective-permute-done.1 = bf16[3,24576]{1,0:T(4,128)(2,1)S(1)} collective-permute-done((bf16[3,24576]{1,0:T(4,128)(2,1)S(1)}, bf16[3,24576]{1,0:T(4,128)(2,1)S(1)}, u32[]{:S(2)}, u32[]{:S(2)}) %collective-permute-start.1) | collective-permute-done | bytes 147488 | tf_op jit(solution)/shard_map/ppermute | solution.py:30
  67.5 36.8 %conditional.11 = (bf16[8,8,1024]{2,1,0:T(8,128)(2,1)}, bf16[16,16,1024]{2,1,0:T(8,128)(2,1)}, bf16[64,64]{1,0:T(8,128)(2,1)S(1)}) conditional(s32[]{:T(128)} %clamp.24, () %tuple.204, (bf16[3,24576]{1,0:T(4,128)(2,1)S(1)}, bf16[3,24576]{1,0:T(4,128)(2,1)S(1)}, bf16[16,16,1024]{2,1,0:T(8,128)(2,1)S(1)}, ...), branch_computations={%region_12.13_spmd, %region_13.15_spmd, %region_15.17_spmd, %regio... | conditional | flops 920126016 | bytes 43903200 | solution.py:335
  91.4 5.6 %fusion.31 = bf16[8,8,1024]{2,1,0:T(8,128)(2,1)} fusion(bf16[64,4096]{1,0:T(8,128)(2,1)S(1)} %reshape.3187, bf16[4096,1024]{1,0:T(8,128)(2,1)} %get-tuple-element.546), kind=kOutput, calls=%fused_computation.86 | convolution fusion | flops 536936448 | bytes 9043968 | tf_op jit(solution)/shard_map/cond/branch_1_fun/dot_general | solution.py:217
  108.1 4.5 %collective-permute-done.3 = bf16[16,16,1024]{2,1,0:T(8,128)(2,1)S(1)} collective-permute-done((bf16[16,16,1024]{2,1,0:T(8,128)(2,1)}, bf16[16,16,1024]{2,1,0:T(8,128)(2,1)S(1)}, u32[]{:S(2)}, u32[]{:S(2)}) %collective-permute-start.3) | collective-permute-done | bytes 524320 | tf_op jit(solution)/shard_map/ppermute | solution.py:38
  113.4 29.6 %conditional.12 = (f32[16,16,1024]{2,1,0:T(8,128)}, bf16[16,16,512]{2,1,0:T(8,128)(2,1)S(1)}, bf16[16,16,1024]{2,1,0:T(8,128)(2,1)S(1)}, f32[8,8,1024]{2,1,0:T(8...) conditional(s32[]{:T(128)} %clamp.23, () %tuple.202, ...), branch_computations={%region_20.21_spmd, %region_21.25_spmd, %region_25.29_spmd, %regio... | conditional | flops 1347129600 | bytes 60207320 | solution.py:278
  150.7 6.1 %collective-permute-done.5 = bf16[3,24576]{1,0:T(4,128)(2,1)S(1)} collective-permute-done((bf16[3,24576]{1,0:T(4,128)(2,1)S(1)}, bf16[3,24576]{1,0:T(4,128)(2,1)S(1)}, u32[]{:S(2)}, u32[]{:S(2)}) %collective-permute-start.5) | collective-permute-done | bytes 147488 | tf_op jit(solution)/shard_map/ppermute | solution.py:30
  156.8 33.8 %conditional.13 = (bf16[8,8,1024]{2,1,0:T(8,128)(2,1)}, bf16[16,16,1024]{2,1,0:T(8,128)(2,1)}, bf16[64,64]{1,0:T(8,128)(2,1)S(1)}) conditional(s32[]{:T(128)} %clamp.23, () %tuple.201, (bf16[3,24576]{1,0:T(4,128)(2,1)S(1)}, bf16[3,24576]{1,0:T(4,128)(2,1)S(1)}, bf16[16,16,1024]{2,1,0:T(8,128)(2,1)S(1)}, ...), branch_computations={%region_33.34_spmd, %region_34.36_spmd, %region_36.38_spmd, %regio... | conditional | flops 920126016 | bytes 49457432 | solution.py:335
  177.7 5.6 %fusion.139 = bf16[8,8,1024]{2,1,0:T(8,128)(2,1)} fusion(bf16[64,4096]{1,0:T(8,128)(2,1)S(1)} %reshape.3209, bf16[4096,1024]{1,0:T(8,128)(2,1)} %get-tuple-element.588), kind=kOutput, calls=%fused_computation.335 | convolution fusion | flops 536936448 | bytes 9043968 | tf_op jit(solution)/shard_map/cond/branch_1_fun/dot_general | solution.py:217
  194.6 4.5 %collective-permute-done.7 = bf16[16,16,1024]{2,1,0:T(8,128)(2,1)S(1)} collective-permute-done((bf16[16,16,1024]{2,1,0:T(8,128)(2,1)}, bf16[16,16,1024]{2,1,0:T(8,128)(2,1)S(1)}, u32[]{:S(2)}, u32[]{:S(2)}) %collective-permute-start.7) | collective-permute-done | bytes 524320 | tf_op jit(solution)/shard_map/ppermute | solution.py:38
  200.2 10.9 %conditional.14 = (f32[16,16,1024]{2,1,0:T(8,128)}, bf16[16,16,512]{2,1,0:T(8,128)(2,1)S(1)}, bf16[16,16,1024]{2,1,0:T(8,128)(2,1)S(1)}, f32[8,8,1024]{2,1,0:T(8...) conditional(s32[]{:T(128)} %clamp.22, () %tuple.199, ...), branch_computations={%region_41.42_spmd, %region_42.46_spmd, %region_46.50_spmd, %regio... | conditional | flops 1347129600 | bytes 60207320 | solution.py:278
  218.9 6.1 %collective-permute-done.9 = bf16[3,24576]{1,0:T(4,128)(2,1)S(1)} collective-permute-done((bf16[3,24576]{1,0:T(4,128)(2,1)S(1)}, bf16[3,24576]{1,0:T(4,128)(2,1)S(1)}, u32[]{:S(2)}, u32[]{:S(2)}) %collective-permute-start.9) | collective-permute-done | bytes 147488 | tf_op jit(solution)/shard_map/ppermute | solution.py:30
  225.0 7.8 %conditional.15 = (bf16[8,8,1024]{2,1,0:T(8,128)(2,1)}, bf16[64,64]{1,0:T(8,128)(2,1)S(1)}) conditional(s32[]{:T(128)} %clamp.22, () %tuple.198, (bf16[3,24576]{1,0:T(4,128)(2,1)S(1)}, bf16[3,24576]{1,0:T(4,128)(2,1)S(1)}, bf16[16,16,1024]{2,1,0:T(8,128)(2,1)S(1)}, bf16[16,16,512]{2,1,0:T(8,128)(2,1)S(1)}, ...), branch_computations={%region_54.55_spmd, %region_55.57_spmd, %region_57.59_spmd, %regio... | conditional | flops 920126016 | bytes 48097520 | solution.py:335
  232.8 24.7 %collective-permute-start.10 = (bf16[8,8,1024]{2,1,0:T(8,128)(2,1)}, bf16[8,8,1024]{2,1,0:T(8,128)(2,1)S(1)}, u32[]{:S(2)}, u32[]{:S(2)}) collective-permute-start(bf16[8,8,1024]{2,1,0:T(8,128)(2,1)} %get-tuple-element.782), channel_id=1, source_target_pairs={{0,64},{64,128},{128,192},{1,65},{65,129},{129,193},{2,66},{66,130... | collective-permute-start | bytes 393224 | tf_op jit(solution)/shard_map/ppermute | solution.py:38
  258.7 10.9 %conditional.16 = (f32[16,16,1024]{2,1,0:T(8,128)}, bf16[16,16,512]{2,1,0:T(8,128)(2,1)S(1)}, bf16[16,16,1024]{2,1,0:T(8,128)(2,1)S(1)}, f32[8,8,1024]{2,1,0:T(8...) conditional(s32[]{:T(128)} %clamp.21, () %tuple.196, ...), branch_computations={%region_62.63_spmd, %region_63.67_spmd, %region_67.71_spmd, %regio... | conditional | flops 1347129600 | bytes 59158688 | solution.py:278
  279.4 6.1 %collective-permute-done.12 = bf16[3,24576]{1,0:T(4,128)(2,1)S(1)} collective-permute-done((bf16[3,24576]{1,0:T(4,128)(2,1)S(1)}, bf16[3,24576]{1,0:T(4,128)(2,1)S(1)}, u32[]{:S(2)}, u32[]{:S(2)}) %collective-permute-start.12) | collective-permute-done | bytes 147488 | tf_op jit(solution)/shard_map/ppermute | solution.py:30
  285.5 7.1 %conditional.17 = (bf16[8,8,1024]{2,1,0:T(8,128)(2,1)}, bf16[64,64]{1,0:T(8,128)(2,1)S(1)}) conditional(s32[]{:T(128)} %clamp.21, () %tuple.195, (bf16[3,24576]{1,0:T(4,128)(2,1)S(1)}, bf16[3,24576]{1,0:T(4,128)(2,1)S(1)}, bf16[16,16,1024]{2,1,0:T(8,128)(2,1)S(1)}, bf16[16,16,512]{2,1,0:T(8,128)(2,1)S(1)}, ...), branch_computations={%region_75.76_spmd, %region_76.78_spmd, %region_78.80_spmd, %regio... | conditional | flops 920126016 | bytes 48097520 | solution.py:335
  295.8 8.0 %conditional.18 = (f32[16,16,1024]{2,1,0:T(8,128)}, bf16[16,16,512]{2,1,0:T(8,128)(2,1)S(1)}, bf16[16,16,1024]{2,1,0:T(8,128)(2,1)}, bf16[6,24576]{1,0:T(8,128)(2,1)}) conditional(s32[]{:T(128)} %clamp.20, () %tuple.193, (s32[]{:T(128)}, f32[2,64,64]{2,1,0:T(8,128)}, f32[2]{0:T(128)}, f32[2,64,64]{2,1,0:T(8,128)}, ...), branch_computations={%region_83.84_spmd, %region_84.88_spmd, %region_88.91_spmd, %regio... | conditional | flops 1347129600 | bytes 58306696 | solution.py:278
  314.3 4.6 %collective-permute-done.15 = bf16[3,24576]{1,0:T(4,128)(2,1)S(1)} collective-permute-done((bf16[3,24576]{1,0:T(4,128)(2,1)S(1)}, bf16[3,24576]{1,0:T(4,128)(2,1)S(1)}, u32[]{:S(2)}, u32[]{:S(2)}) %collective-permute-start.15) | collective-permute-done | bytes 147488 | tf_op jit(solution)/shard_map/ppermute | solution.py:30
  319.1 85.2 %psum.7 = bf16[2,64,64]{1,2,0:T(8,128)(2,1)S(1)} all-reduce(bf16[2,64,64]{1,2,0:T(8,128)(2,1)S(1)} %fusion.491), channel_id=1, replica_groups=mesh['segment'=4,'space'=64] {'segment'}, use_global_device_ids=true, to_apply=%region_101.102 | all-reduce | flops 8192 | bytes 32768 | tf_op jit(solution)/shard_map/psum | solution.py:43
  (270 shorter events, 146.7 us)
Async XLA Ops:
  0.0 23.4 %copy-start = (bf16[1,256,1024]{2,1,0:T(8,128)(2,1)S(1)}, bf16[1,256,1024]{2,1,0:T(8,128)(2,1)}, u32[]{:S(2)}) copy-start(bf16[1,256,1024]{2,1,0:T(8,128)(2,1)} %param.59) | copy-start | bytes 1572868
  51.0 8.5 %collective-permute-start = (bf16[3,24576]{1,0:T(4,128)(2,1)S(1)}, bf16[3,24576]{1,0:T(4,128)(2,1)S(1)}, u32[]{:S(2)}, u32[]{:S(2)}) collective-permute-start(bf16[3,24576]{1,0:T(4,128)(2,1)S(1)} %get-tuple-element.1201), channel_id=1, source_target_pairs={{0,1},{1,2},{2,3},{3,4},{4,5},{5,6},{6,7},{7,8},{8,9},{9,10},{10,1... | collective-permute-start | bytes 442376 | tf_op jit(solution)/shard_map/ppermute | solution.py:29
  55.6 11.8 %collective-permute-start.1 = (bf16[3,24576]{1,0:T(4,128)(2,1)S(1)}, bf16[3,24576]{1,0:T(4,128)(2,1)S(1)}, u32[]{:S(2)}, u32[]{:S(2)}) collective-permute-start(bf16[3,24576]{1,0:T(4,128)(2,1)S(1)} %get-tuple-element.1200), channel_id=1, source_target_pairs={{1,0},{2,1},{3,2},{4,3},{5,4},{6,5},{7,6},{8,7},{9,8},{10,9},{11,1... | collective-permute-start | bytes 442376 | tf_op jit(solution)/shard_map/ppermute | solution.py:30
  104.3 8.3 %collective-permute-start.3 = (bf16[16,16,1024]{2,1,0:T(8,128)(2,1)}, bf16[16,16,1024]{2,1,0:T(8,128)(2,1)S(1)}, u32[]{:S(2)}, u32[]{:S(2)}) collective-permute-start(bf16[16,16,1024]{2,1,0:T(8,128)(2,1)} %get-tuple-element.765), channel_id=1, source_target_pairs={{0,192},{1,193},{2,194},{3,195},{4,196},{5,197},{6,198},{7,199},{8... | collective-permute-start | bytes 1572872 | tf_op jit(solution)/shard_map/ppermute | solution.py:38
  105.6 2.5 collective-permute-start.2
  112.6 44.2 %copy-start.107 = (f32[1,24]{1,0:T(1,128)S(1)}, f32[1,24]{1,0:T(1,128)}, u32[]{:S(2)}) copy-start(f32[1,24]{1,0:T(1,128)} %param.63) | copy-start | bytes 292
  143.1 7.6 %collective-permute-start.4 = (bf16[3,24576]{1,0:T(4,128)(2,1)S(1)}, bf16[3,24576]{1,0:T(4,128)(2,1)S(1)}, u32[]{:S(2)}, u32[]{:S(2)}) collective-permute-start(bf16[3,24576]{1,0:T(4,128)(2,1)S(1)} %get-tuple-element.1199), channel_id=1, source_target_pairs={{0,1},{1,2},{2,3},{3,4},{4,5},{5,6},{6,7},{7,8},{8,9},{9,10},{10,1... | collective-permute-start | bytes 442376 | tf_op jit(solution)/shard_map/ppermute | solution.py:29
  145.0 11.8 %collective-permute-start.5 = (bf16[3,24576]{1,0:T(4,128)(2,1)S(1)}, bf16[3,24576]{1,0:T(4,128)(2,1)S(1)}, u32[]{:S(2)}, u32[]{:S(2)}) collective-permute-start(bf16[3,24576]{1,0:T(4,128)(2,1)S(1)} %get-tuple-element.1198), channel_id=1, source_target_pairs={{1,0},{2,1},{3,2},{4,3},{5,4},{6,5},{7,6},{8,7},{9,8},{10,9},{11,1... | collective-permute-start | bytes 442376 | tf_op jit(solution)/shard_map/ppermute | solution.py:30
  156.8 42.3 %copy-start.41 = (bf16[16,16,1024]{2,1,0:T(8,128)(2,1)S(1)}, bf16[16,16,1024]{2,1,0:T(8,128)(2,1)}, u32[]{:S(2)}) copy-start(bf16[16,16,1024]{2,1,0:T(8,128)(2,1)} %copy-done.40) | copy-start | bytes 1572868
  190.7 8.4 %collective-permute-start.7 = (bf16[16,16,1024]{2,1,0:T(8,128)(2,1)}, bf16[16,16,1024]{2,1,0:T(8,128)(2,1)S(1)}, u32[]{:S(2)}, u32[]{:S(2)}) collective-permute-start(bf16[16,16,1024]{2,1,0:T(8,128)(2,1)} %get-tuple-element.774), channel_id=1, source_target_pairs={{0,192},{1,193},{2,194},{3,195},{4,196},{5,197},{6,198},{7,199},{8... | collective-permute-start | bytes 1572872 | tf_op jit(solution)/shard_map/ppermute | solution.py:38
  192.1 2.5 collective-permute-start.6
  200.2 24.8 %copy-start.108 = (s32[1,1,9]{2,1,0:T(1,128)S(1)}, s32[1,1,9]{2,1,0:T(1,128)}, u32[]{:S(2)}) copy-start(s32[1,1,9]{2,1,0:T(1,128)} %param.65) | copy-start | bytes 112
  211.3 7.6 %collective-permute-start.8 = (bf16[3,24576]{1,0:T(4,128)(2,1)S(1)}, bf16[3,24576]{1,0:T(4,128)(2,1)S(1)}, u32[]{:S(2)}, u32[]{:S(2)}) collective-permute-start(bf16[3,24576]{1,0:T(4,128)(2,1)S(1)} %get-tuple-element.1197), channel_id=1, source_target_pairs={{0,1},{1,2},{2,3},{3,4},{4,5},{5,6},{6,7},{7,8},{8,9},{9,10},{10,1... | collective-permute-start | bytes 442376 | tf_op jit(solution)/shard_map/ppermute | solution.py:29
  213.2 11.8 %collective-permute-start.9 = (bf16[3,24576]{1,0:T(4,128)(2,1)S(1)}, bf16[3,24576]{1,0:T(4,128)(2,1)S(1)}, u32[]{:S(2)}, u32[]{:S(2)}) collective-permute-start(bf16[3,24576]{1,0:T(4,128)(2,1)S(1)} %get-tuple-element.1196), channel_id=1, source_target_pairs={{1,0},{2,1},{3,2},{4,3},{5,4},{6,5},{7,6},{8,7},{9,8},{10,9},{11,1... | collective-permute-start | bytes 442376 | tf_op jit(solution)/shard_map/ppermute | solution.py:30
  225.0 33.7 %copy-start.67 = (f32[16,1024]{1,0:T(8,128)S(1)}, f32[16,1024]{1,0:T(8,128)}, u32[]{:S(2)}) copy-start(f32[16,1024]{1,0:T(8,128)} %param.60) | copy-start | bytes 196612
  225.0 33.7 %copy-start.93 = (f32[1,1024]{1,0:T(1,128)S(1)}, f32[1,1024]{1,0:T(1,128)}, u32[]{:S(2)}) copy-start(f32[1,1024]{1,0:T(1,128)} %get-tuple-element.1206) | copy-start | bytes 12292
  232.8 25.9 %copy-start.101 = (bf16[64,64]{1,0:T(8,128)(2,1)}, bf16[64,64]{1,0:T(8,128)(2,1)S(1)}, u32[]{:S(2)}) copy-start(bf16[64,64]{1,0:T(8,128)(2,1)S(1)} %get-tuple-element.796) | copy-start | bytes 24580
  232.8 25.9 %collective-permute-start.10 = (bf16[8,8,1024]{2,1,0:T(8,128)(2,1)}, bf16[8,8,1024]{2,1,0:T(8,128)(2,1)S(1)}, u32[]{:S(2)}, u32[]{:S(2)}) collective-permute-start(bf16[8,8,1024]{2,1,0:T(8,128)(2,1)} %get-tuple-element.782), channel_id=1, source_target_pairs={{0,64},{64,128},{128,192},{1,65},{65,129},{129,193},{2,66},{66,130... | collective-permute-start | bytes 393224 | tf_op jit(solution)/shard_map/ppermute | solution.py:38
  269.8 9.6 %collective-permute-start.11 = (bf16[3,24576]{1,0:T(4,128)(2,1)S(1)}, bf16[3,24576]{1,0:T(4,128)(2,1)S(1)}, u32[]{:S(2)}, u32[]{:S(2)}) collective-permute-start(bf16[3,24576]{1,0:T(4,128)(2,1)S(1)} %get-tuple-element.1195), channel_id=1, source_target_pairs={{0,1},{1,2},{2,3},{3,4},{4,5},{5,6},{6,7},{7,8},{8,9},{9,10},{10,1... | collective-permute-start | bytes 442376 | tf_op jit(solution)/shard_map/ppermute | solution.py:29
  271.7 13.8 %collective-permute-start.12 = (bf16[3,24576]{1,0:T(4,128)(2,1)S(1)}, bf16[3,24576]{1,0:T(4,128)(2,1)S(1)}, u32[]{:S(2)}, u32[]{:S(2)}) collective-permute-start(bf16[3,24576]{1,0:T(4,128)(2,1)S(1)} %get-tuple-element.1194), channel_id=1, source_target_pairs={{1,0},{2,1},{3,2},{4,3},{5,4},{6,5},{7,6},{8,7},{9,8},{10,9},{11,1... | collective-permute-start | bytes 442376 | tf_op jit(solution)/shard_map/ppermute | solution.py:30
  292.6 3.2 collective-permute-start.13
  305.2 9.1 %collective-permute-start.14 = (bf16[3,24576]{1,0:T(4,128)(2,1)S(1)}, bf16[3,24576]{1,0:T(4,128)(2,1)S(1)}, u32[]{:S(2)}, u32[]{:S(2)}) collective-permute-start(bf16[3,24576]{1,0:T(4,128)(2,1)S(1)} %get-tuple-element.1193), channel_id=1, source_target_pairs={{0,1},{1,2},{2,3},{3,4},{4,5},{5,6},{6,7},{7,8},{8,9},{9,10},{10,1... | collective-permute-start | bytes 442376 | tf_op jit(solution)/shard_map/ppermute | solution.py:29
  307.1 11.8 %collective-permute-start.15 = (bf16[3,24576]{1,0:T(4,128)(2,1)S(1)}, bf16[3,24576]{1,0:T(4,128)(2,1)S(1)}, u32[]{:S(2)}, u32[]{:S(2)}) collective-permute-start(bf16[3,24576]{1,0:T(4,128)(2,1)S(1)} %get-tuple-element.1192), channel_id=1, source_target_pairs={{1,0},{2,1},{3,2},{4,3},{5,4},{6,5},{7,6},{8,7},{9,8},{10,9},{11,1... | collective-permute-start | bytes 442376 | tf_op jit(solution)/shard_map/ppermute | solution.py:30
  318.9 86.0 %copy-start.1 = (bf16[1,256,1024]{2,1,0:T(8,128)(2,1)S(1)}, bf16[1,256,1024]{2,1,0:T(8,128)(2,1)}, u32[]{:S(2)}) copy-start(bf16[1,256,1024]{2,1,0:T(8,128)(2,1)} %param.59) | copy-start | bytes 1572868
  (34 other events, 238.9 us)
where the time goes:
time: 414 us; the launch traced here: 405 us
  local copies, waits for them, and re-layouts  85.5 us (21%)
  blocking collectives  85.2 us (21%)
  loops' own time  69.4 us (17%)
  starting transfers between devices  62.1 us (15%)
  waiting for transfers between devices  51.7 us (12%)
  matrix products  35.1 us (8%)
  other arithmetic  15.5 us (4%)
    psum x1, blocking collectives, broadcast(): return lax.psum(kept, axis)  85.2 us
    another operation x5, loops' own time, per_device(): lax.switch(selector, [spare_front, first_front, middle_front, last_front])  40.9 us
    ppermute x6, starting transfers between devices, shifted(): return lax.ppermute(block, axis, route)  32.1 us
    ppermute x5, waiting for transfers between devices, padded_2(): after = lax.ppermute(leading, axis, down)  31 us
    another operation x5, loops' own time, per_device(): lax.switch(selector, [spare_back, first_back, middle_back, last_back])  28.4 us
    ppermute x5, starting transfers between devices, padded_2(): after = lax.ppermute(leading, axis, down)  17.6 us
    ppermute x6, waiting for transfers between devices, shifted(): return lax.ppermute(block, axis, route)  13.6 us
    another operation x30, local copies, waits for them, and re-layouts  12.7 us
  transfers between devices with their start and end apart: 16, of which 14 were waited for; matrix products, arithmetic and copies ran while one was open for 1% of the time, Pallas kernels for 0%

commit v1 on v0

v1 whole, which is shorter than its diff:
```python
import functools
import math

import jax
import jax.numpy as jnp
from jax import lax
from jax.experimental import pallas as pl
from jax.experimental.pallas import tpu as pltpu
from jax.sharding import PartitionSpec as P

STEPS = 1000
MB = 2
D = 1024
FI = 512
CI = 1536
G = 256
OWN = 256
FINE = 384
COWN = 64
COARSE = 128
EPS = 1e-06

LOG_LOW = math.log(0.002)
LOG_HIGH = math.log(80.0)
LOG2E = 1.0 / math.log(2.0)

F32 = jnp.float32
BF16 = jnp.bfloat16
NT = (((1,), (1,)), ((), ()))
NN = (((1,), (0,)), ((), ()))

CHUNK = 512
CHUNKS = 12


def dot_nt(a, b):
    return lax.dot_general(a, b, NT, preferred_element_type=F32)


def dot_nn(a, b):
    return lax.dot_general(a, b, NN, preferred_element_type=F32)


def iota(shape, dim):
    return lax.broadcasted_iota(jnp.int32, shape, dim)


def split3(value):
    hi = value.astype(BF16)
    rest = value - hi.astype(F32)
    mid = rest.astype(BF16)
    return hi, mid, (rest - mid.astype(F32)).astype(BF16)


def kernel(
    n_space,
    frames, noise, steps, freqs, cond, patch_in, patch_out, w_hbm, scales, fine_links, coarse_links,
    out,
    w, xs, x, nrm, q_s, k_s, v_s, mix, grp, skip, cin, cout, w3, pox, gains, qscale, links, fmask, cmask, pixout, pixin,
    w_sem, halo_s, halo_r, link_s, link_r, c_s, c_r, skip_s, skip_r, fwd_s, fwd_r, pix_s, pix_r,
):
    s = lax.axis_index("segment")
    p = lax.axis_index("space")
    b = p + (s // 2) * (1 - 2 * (p % 2))
    has_up = b > 0
    has_down = b < n_space - 1

    def place(seg, block):
        return block + (seg // 2) * (1 - 2 * (block % 2))

    def remote(src, dst, ssem, rsem, seg, block):
        return pltpu.make_async_remote_copy(
            src_ref=src, dst_ref=dst, send_sem=ssem, recv_sem=rsem,
            device_id=(seg, place(seg, block)), device_id_type=pl.DeviceIdType.MESH,
        )

    def arrived(dst, rsem):
        pltpu.make_async_remote_copy(
            src_ref=dst, dst_ref=dst, send_sem=rsem, recv_sem=rsem,
            device_id=(s, p), device_id_type=pl.DeviceIdType.MESH,
        ).wait_recv()

    def weight_copy(i):
        return pltpu.make_async_copy(
            w_hbm.at[0, pl.ds(i * CHUNK, CHUNK), :], w.at[pl.ds(i * CHUNK, CHUNK), :], w_sem.at[i]
        )

    barrier = pltpu.get_barrier_semaphore()

    def greet(seg, space):
        pl.semaphore_signal(barrier, inc=1, device_id=(seg, space), device_id_type=pl.DeviceIdType.MESH)

    greet(3, place(3, p))

    @pl.when(s > 0)
    def _():
        greet(s - 1, place(s - 1, b))

        @pl.when(has_up)
        def _():
            greet(s - 1, place(s - 1, b - 1))

        @pl.when(has_down)
        def _():
            greet(s - 1, place(s - 1, b + 1))

    @pl.when((s == 0) | (s == 3))
    def _():
        @pl.when(has_up)
        def _():
            greet(s, place(s, b - 1))

        @pl.when(has_down)
        def _():
            greet(s, place(s, b + 1))

    @pl.when(s == 3)
    def _():
        greet(0, b)

    for i in range(CHUNKS):
        weight_copy(i).start()

    def level_row(m):
        step = jnp.full((1, 128), steps[m], jnp.int32).astype(F32)
        return jnp.exp(LOG_LOW + step / (STEPS - 1) * (LOG_HIGH - LOG_LOW))

    freq_row = freqs[...].reshape(1, 128)
    rows = []
    for m in range(MB):
        phases = 2.0 * math.pi * (jnp.log(level_row(m)) / 4.0) * freq_row
        rows.append(jnp.concatenate([jnp.cos(phases), jnp.sin(phases)], axis=1))
    features = jnp.concatenate(rows + [jnp.zeros((6, 256), F32)], axis=0)
    hi, mid, low = split3(features)
    gains[...] = 1.0 + (dot_nn(hi, cond[0]) + dot_nn(mid, cond[0]) + dot_nn(low, cond[0]))

    lane = iota((1, G), 1) // 64
    for g in range(6):
        four = [scales[0, 4 * g + h] for h in range(4)]
        row = jnp.where(lane == 0, four[0], jnp.where(lane == 1, four[1], jnp.where(lane == 2, four[2], four[3])))
        qscale[g : g + 1, :] = row * (LOG2E / 64.0)

    head_mean = jnp.where(iota((G, G), 0) // 64 == iota((G, G), 1) // 64, 1.0 / 64.0, 0.0).astype(BF16)
    ones = jnp.ones((G, 128), BF16)

    @pl.when(s == 0)
    def _():
        key = iota((1, 256), 1)
        key_row = key // 16
        key_tile = (key % 8) // 4
        for t in range(2):
            for c in range(2):
                row = jnp.zeros((1, 256), F32)
                for dy in range(3):
                    in_row = (key_row >= (0, 4, 12)[dy]) & (key_row < (4, 12, 16)[dy])
                    for kc in range(2):
                        link = fine_links[t, c, 3 * dy + kc - c + 1].astype(F32)
                        row = jnp.where(in_row & (key_tile == kc), link, row)
                links[2 * t + c : 2 * t + c + 1, :] = row

    @pl.when(s == 1)
    def _():
        key_row = iota((1, 256), 1) // 8
        row = jnp.zeros((1, 256), F32)
        for dy in range(3):
            in_row = (key_row >= (0, 4, 12)[dy]) & (key_row < (4, 12, 16)[dy])
            row = jnp.where(in_row, coarse_links[0, 0, 3 * dy + 1].astype(F32), row)
        links[0:1, :] = row

    def make_fine_mask():
        query = iota((128, 256), 0)
        key = iota((128, 256), 1)
        row_gap = key // 16 - 4 - query // 16
        query_col = 2 * (query % 8) + (query // 8) % 2
        key_col = 2 * (key % 8) + (key // 8) % 2
        col_gap = key_col - query_col
        near = (row_gap <= 3) & (row_gap >= -3) & (col_gap <= 3) & (col_gap >= -3)
        for t in range(2):
            left = jnp.broadcast_to(links[2 * t : 2 * t + 1, :], (128, 256))
            right = jnp.broadcast_to(links[2 * t + 1 : 2 * t + 2, :], (128, 256))
            value = jnp.where(query_col < 8, left, right)
            fmask[t] = jnp.where(near, value, 0.0).astype(BF16)

    def make_coarse_mask():
        query = iota((64, 128), 0)
        key = iota((64, 128), 1)
        row_gap = key // 8 - 4 - query // 8
        col_gap = key % 8 - query % 8
        near = (row_gap <= 3) & (row_gap >= -3) & (col_gap <= 3) & (col_gap >= -3)
        value = jnp.broadcast_to(links[0:1, 0:128], (64, 128))
        cmask[...] = jnp.where(near, value, 0.0).astype(BF16)

    @pl.when(s == 0)
    def _():
        for m in range(MB):
            level = level_row(m)[:, 0:64]
            scaled = (frames[m] + level * noise[m]) * lax.rsqrt(level * level + 0.25)
            xs[m, 16:80, :] = jnp.concatenate([scaled, jnp.zeros((64, 64), F32)], axis=1)

        @pl.when(b == 0)
        def _():
            xs[:, 0:16, :] = jnp.zeros((MB, 16, 128), F32)

        @pl.when(b == n_space - 1)
        def _():
            xs[:, 80:96, :] = jnp.zeros((MB, 16, 128), F32)

    @pl.when((s == 1) | (s == 2))
    def _():
        @pl.when(b == 0)
        def _():
            cin[:, 0:32, :] = jnp.zeros((MB, 32, D), BF16)

        @pl.when(b == n_space - 1)
        def _():
            cin[:, 96:128, :] = jnp.zeros((MB, 32, D), BF16)

    @pl.when(s == 3)
    def _():
        @pl.when(b == 0)
        def _():
            cin[:, 16:32, :] = jnp.zeros((MB, 16, D), BF16)
            skip[:, 0:64, :] = jnp.zeros((MB, 64, D), BF16)

        @pl.when(b == n_space - 1)
        def _():
            cin[:, 96:112, :] = jnp.zeros((MB, 16, D), BF16)
            skip[:, 320:384, :] = jnp.zeros((MB, 64, D), BF16)

    edges = has_up.astype(jnp.int32) + has_down.astype(jnp.int32)
    for seg, targets in ((0, 2 + 2 * edges), (1, 1 + edges), (2, 1 + edges), (3, 4 + edges)):

        @pl.when(s == seg)
        def _():
            pl.semaphore_wait(barrier, targets)

    def halo_up():
        return remote(xs.at[:, pl.ds(16, 16), :], xs.at[:, pl.ds(80, 16), :], halo_s.at[0], halo_r.at[1], 0, b - 1)

    def halo_down():
        return remote(xs.at[:, pl.ds(64, 16), :], xs.at[:, pl.ds(0, 16), :], halo_s.at[1], halo_r.at[0], 0, b + 1)

    def link_copy(seg):
        return remote(links, links, link_s, link_r, seg, b)

    @pl.when(s == 0)
    def _():
        @pl.when(has_up)
        def _():
            halo_up().start()

        @pl.when(has_down)
        def _():
            halo_down().start()

        link_copy(3).start()
        make_fine_mask()

        entry = iota((256, 16), 0)
        pick = (iota((256, 16), 1) == 4 * (entry // 64) + entry % 4).astype(BF16)
        hi, low, _ = split3(patch_in[...])
        wide = dot_nn(pick, hi).astype(BF16)
        w3[0:256, :] = wide
        w3[256:512, :] = dot_nn(pick, low).astype(BF16)
        w3[512:768, :] = wide

        @pl.when(has_up)
        def _():
            arrived(xs.at[:, pl.ds(0, 16), :], halo_r.at[0])

        @pl.when(has_down)
        def _():
            arrived(xs.at[:, pl.ds(80, 16), :], halo_r.at[1])

    @pl.when(s == 1)
    def _():
        link_copy(2).start()
        make_coarse_mask()

    @pl.when(s == 2)
    def _():
        arrived(links, link_r)
        make_coarse_mask()

    @pl.when(s == 3)
    def _():
        arrived(links, link_r)
        make_fine_mask()
        entry = iota((16, 256), 0)
        col = iota((16, 256), 1)
        pick = (entry == 4 * ((col // 16) % 4) + col % 4).astype(BF16)
        pox[...] = dot_nn(patch_out[...], pick).astype(BF16)

    @pl.when(s == 0)
    def _():
        for i in range(4):
            weight_copy(i).wait()

    @pl.when(s > 0)
    def _():
        for i in range(CHUNKS):
            weight_copy(i).wait()

    def project(source, rows_q, rows_kv, inner):
        groups = inner // G
        for part, dst in ((0, q_s), (1, k_s), (2, v_s)):
            first, count = rows_q if part == 0 else rows_kv
            for g in range(groups):
                at = part * inner + g * G
                block = dot_nt(source[first : first + count, :], w[at : at + G, :])
                if part < 2:
                    power = dot_nn((block * block).astype(BF16), head_mean)
                    block = block * lax.rsqrt(power + EPS)
                if part == 0:
                    block = block * qscale[g : g + 1, :]
                dst[g, 0:count, :] = block.astype(BF16)

    def attend(queries, keys, values, mask, count):
        head = iota((count, G), 1) // 64
        stacked = jnp.concatenate(
            [jnp.where(head == h, queries, jnp.zeros_like(queries)) for h in range(4)], axis=0
        )
        expo = jnp.exp2(dot_nt(stacked, keys)).astype(BF16)
        expo = expo * jnp.concatenate([mask] * 4, axis=0)
        mixed = dot_nn(expo, values)
        total = dot_nn(expo, ones[0 : keys.shape[0], :])
        part = [mixed[h * count : (h + 1) * count] for h in range(4)]
        sums = [total[h * count : (h + 1) * count] for h in range(4)]
        left = head[:, 0:128] == 0
        right = head[:, 0:128] == 0
        number = jnp.concatenate(
            [
                jnp.where(left, part[0][:, 0:128], part[1][:, 0:128]),
                jnp.where(right, part[2][:, 128:256], part[3][:, 128:256]),
            ],
            axis=1,
        )
        weight = jnp.concatenate(
            [jnp.where(left, sums[0], sums[1]), jnp.where(right, sums[2], sums[3])], axis=1
        )
        return (number / weight).astype(BF16)

    def normed(value, m):
        scale = lax.rsqrt(jnp.mean(value * value, axis=-1, keepdims=True) + EPS)
        return (value * scale * gains[pl.ds(m, 1), :]).astype(BF16)

    def embed(m):
        rows4 = [xs[m, pl.ds(a, 24, stride=4), :] for a in range(4)]
        flat = jnp.concatenate(
            [rows4[0] + pltpu.roll(rows4[1], 64, 1), rows4[2] + pltpu.roll(rows4[3], 64, 1)], axis=1
        )
        hi, low, _ = split3(flat)
        token = iota((16, 256), 0)
        col = iota((16, 256), 1)
        own = ((col % 64) // 4 == 2 * (token % 8) + token // 8).astype(F32)

        def spread(piece):
            wide = jnp.broadcast_to(piece.astype(F32)[:, None, :], (24, 16, 256)) * own[None]
            return wide.reshape(FINE, 256).astype(BF16)

        first = spread(hi)
        lhs = jnp.concatenate([first, first, spread(low)], axis=1)
        x[...] = dot_nn(lhs, w3[...]).reshape(12, 2, 2, 8, D)

    def widen(m):
        coarse = cin[m, 16:112, :]
        for a in range(2):
            for c in range(2):
                at = 4 * FI + (2 * a + c) * D
                x[:, a, c] = dot_nt(coarse, w[at : at + D, :]).reshape(12, 8, D)
        x[...] += skip[m].astype(F32).reshape(12, 2, 2, 8, D)

    def fine_block(m):
        nrm[...] = normed(x[...].reshape(FINE, D), m)
        project(nrm, (64, OWN), (0, FINE), FI)
        for t in range(2):
            for g in range(2):
                mix[128 * t : 128 * t + 128, g * G : (g + 1) * G] = attend(
                    q_s[g, 128 * t : 128 * t + 128, :],
                    k_s[g, 128 * t : 128 * t + 256, :],
                    v_s[g, 128 * t : 128 * t + 256, :],
                    fmask[t],
                    128,
                )
        update = dot_nn(mix[:, 0:FI], w[3 * FI : 4 * FI, :])
        x[2:10] += update.reshape(8, 2, 2, 8, D)

    def coarse_block(m):
        nrm[0:COARSE, :] = normed(cin[m].astype(F32), m)
        project(nrm, (32, COWN), (0, COARSE), CI)
        for g in range(6):
            mix[0:COWN, g * G : (g + 1) * G] = attend(
                q_s[g, 0:COWN, :], k_s[g, 0:COARSE, :], v_s[g, 0:COARSE, :], cmask[...], COWN
            )
        update = dot_nn(mix[0:COWN, :], w[3 * CI : 4 * CI, :])
        cout[m] = (cin[m, 32:96, :].astype(F32) + update).astype(BF16)

    def merge(m):
        own = x[2:10]
        skip[m, 64:320, :] = own.reshape(OWN, D).astype(BF16)
        for a in range(2):
            for c in range(2):
                at = (2 * a + c) * D
                grp[:, at : at + D] = own[:, a, c].reshape(COWN, D).astype(BF16)

        @pl.when(m == 0)
        def _():
            for i in range(4, CHUNKS):
                weight_copy(i).wait()

        cout[m] = dot_nn(grp[...], w[4 * FI :, :]).astype(BF16)

    def head(m):
        top = x[2:10].reshape(OWN, D)
        scale = lax.rsqrt(jnp.mean(top * top, axis=-1, keepdims=True) + EPS)
        pixels = dot_nn((top * scale).astype(BF16), pox[...])
        token = iota((16, 256), 0)
        col = iota((16, 256), 1)
        own = 2 * (token % 8) + token // 8 == 4 * (col // 64) + (col // 4) % 4
        spread = jnp.where(own[None], pixels.reshape(16, 16, 256), 0.0)
        placed = jnp.sum(spread, axis=1)
        pixout[m, 0] = placed[:, 0:128]
        pixout[m, 1] = placed[:, 128:256]

    def coarse_own(m, seg):
        return remote(cout.at[m], cin.at[m, pl.ds(32, 64), :], c_s.at[m, 0], c_r.at[m, 0], seg + 1, b)

    def coarse_up(m, seg, rows):
        return remote(
            cout.at[m, pl.ds(0, rows), :], cin.at[m, pl.ds(96, rows), :], c_s.at[m, 1], c_r.at[m, 2], seg + 1, b - 1
        )

    def coarse_down(m, seg, rows):
        return remote(
            cout.at[m, pl.ds(64 - rows, rows), :], cin.at[m, pl.ds(32 - rows, rows), :],
            c_s.at[m, 2], c_r.at[m, 1], seg + 1, b + 1,
        )

    def send_coarse(m, seg, rows, act):
        @pl.when(has_up)
        def _():
            act(coarse_up(m, seg, rows))

        @pl.when(has_down)
        def _():
            act(coarse_down(m, seg, rows))

        act(coarse_own(m, seg))

    def take_coarse(m, rows):
        arrived(cin.at[m, pl.ds(32, 64), :], c_r.at[m, 0])

        @pl.when(has_up)
        def _():
            arrived(cin.at[m, pl.ds(32 - rows, rows), :], c_r.at[m, 1])

        @pl.when(has_down)
        def _():
            arrived(cin.at[m, pl.ds(96, rows), :], c_r.at[m, 2])

    def skip_copy(m):
        return remote(
            skip.at[m, pl.ds(64, OWN), :], skip.at[m, pl.ds(64, OWN), :], skip_s.at[m], skip_r.at[m], 3, b
        )

    def skip_up(m):
        return remote(
            skip.at[m, pl.ds(64, 64), :], skip.at[m, pl.ds(320, 64), :], fwd_s.at[m, 0], fwd_r.at[m, 1], 3, b - 1
        )

    def skip_down(m):
        return remote(
            skip.at[m, pl.ds(256, 64), :], skip.at[m, pl.ds(0, 64), :], fwd_s.at[m, 1], fwd_r.at[m, 0], 3, b + 1
        )

    def forward_skip(m, act):
        @pl.when(has_up)
        def _():
            act(skip_up(m))

        @pl.when(has_down)
        def _():
            act(skip_down(m))

    def pixel_copy(m, seg):
        return pltpu.make_async_remote_copy(
            src_ref=pixout.at[m, seg // 2], dst_ref=pixin.at[m], send_sem=pix_s.at[m, seg], recv_sem=pix_r.at[m],
            device_id=(seg, b), device_id_type=pl.DeviceIdType.MESH,
        )

    def start(copy):
        copy.start()

    def sent(copy):
        copy.wait_send()

    def one_batch(m, carry):
        @pl.when(s == 0)
        def _():
            embed(m)

        @pl.when(s == 3)
        def _():
            @pl.when(m == 0)
            def _():
                arrived(skip.at[0, pl.ds(64, OWN), :], skip_r.at[0])
                forward_skip(0, start)

            take_coarse(m, 16)

            @pl.when(has_up)
            def _():
                arrived(skip.at[m, pl.ds(0, 64), :], fwd_r.at[m, 0])

            @pl.when(has_down)
            def _():
                arrived(skip.at[m, pl.ds(320, 64), :], fwd_r.at[m, 1])

            widen(m)

            @pl.when(m == 0)
            def _():
                arrived(skip.at[1, pl.ds(64, OWN), :], skip_r.at[1])
                forward_skip(1, start)

        @pl.when((s == 0) | (s == 3))
        def _():
            fine_block(m)

        @pl.when(s == 0)
        def _():
            merge(m)
            send_coarse(m, 0, 32, start)
            skip_copy(m).start()

        @pl.when(s == 3)
        def _():
            head(m)
            for seg in range(4):
                pixel_copy(m, seg).start()

        @pl.when((s == 1) | (s == 2))
        def _():
            take_coarse(m, 32)
            coarse_block(m)

        @pl.when(s == 1)
        def _():
            send_coarse(m, 1, 32, start)

        @pl.when(s == 2)
        def _():
            send_coarse(m, 2, 16, start)

        return carry

    lax.fori_loop(0, MB, one_batch, 0)

    for m in range(MB):
        arrived(pixin.at[m], pix_r.at[m])
        pixels = pixin[m]
        pixels = jnp.where(s % 2 == 1, pltpu.roll(pixels, 64, 1), pixels)
        for a in range(4):
            out[m, pl.ds(a, 16, stride=4), :] = pixels[:, 16 * a : 16 * a + 16]

    @pl.when(s == 0)
    def _():
        @pl.when(has_up)
        def _():
            halo_up().wait_send()

        @pl.when(has_down)
        def _():
            halo_down().wait_send()

        link_copy(3).wait_send()
        for m in range(MB):
            send_coarse(m, 0, 32, sent)
            skip_copy(m).wait_send()

    @pl.when(s == 1)
    def _():
        link_copy(2).wait_send()
        for m in range(MB):
            send_coarse(m, 1, 32, sent)

    @pl.when(s == 2)
    def _():
        for m in range(MB):
            send_coarse(m, 2, 16, sent)

    @pl.when(s == 3)
    def _():
        for m in range(MB):
            forward_skip(m, sent)
            for seg in range(4):
                pixel_copy(m, seg).wait_send()


def per_device(
    clean_frames, noise, noise_steps, noise_freqs, cond_weights, patch_in, patch_out, section_weights, head_scales,
    fine_links, coarse_links,
):
    vmem = pl.BlockSpec(memory_space=pltpu.VMEM)
    smem = pl.BlockSpec(memory_space=pltpu.SMEM)
    hbm = pl.BlockSpec(memory_space=pl.ANY)
    dma = pltpu.SemaphoreType.DMA
    return pl.pallas_call(
        functools.partial(kernel, lax.axis_size("space")),
        out_shape=jax.ShapeDtypeStruct((MB, 64, 16), F32),
        in_specs=[vmem, vmem, smem, vmem, vmem, vmem, vmem, hbm, smem, smem, smem],
        out_specs=vmem,
        scratch_shapes=[
            pltpu.VMEM((6144, D), BF16),
            pltpu.VMEM((MB, 96, 128), F32),
            pltpu.VMEM((12, 2, 2, 8, D), F32),
            pltpu.VMEM((FINE, D), BF16),
            pltpu.VMEM((6, OWN, G), BF16),
            pltpu.VMEM((6, FINE, G), BF16),
            pltpu.VMEM((6, FINE, G), BF16),
            pltpu.VMEM((OWN, CI), BF16),
            pltpu.VMEM((COWN, 4 * D), BF16),
            pltpu.VMEM((MB, FINE, D), BF16),
            pltpu.VMEM((MB, COARSE, D), BF16),
            pltpu.VMEM((MB, COWN, D), BF16),
            pltpu.VMEM((768, D), BF16),
            pltpu.VMEM((D, 256), BF16),
            pltpu.VMEM((8, D), F32),
            pltpu.VMEM((8, G), F32),
            pltpu.VMEM((8, 256), F32),
            pltpu.VMEM((2, 128, 256), BF16),
            pltpu.VMEM((64, 128), BF16),
            pltpu.VMEM((MB, 2, 16, 128), F32),
            pltpu.VMEM((MB, 16, 128), F32),
            dma((CHUNKS,)),
            dma((2,)), dma((2,)),
            dma(()), dma(()),
            dma((MB, 3)), dma((MB, 3)),
            dma((MB,)), dma((MB,)),
            dma((MB, 2)), dma((MB, 2)),
            dma((MB, 4)), dma((MB,)),
        ],
        compiler_params=pltpu.CompilerParams(
            collective_id=0, has_side_effects=True, vmem_limit_bytes=56 << 20
        ),
    )(
        clean_frames, noise, noise_steps, noise_freqs, cond_weights, patch_in, patch_out, section_weights,
        head_scales, fine_links, coarse_links,
    )


def solution(mesh):
    in_specs = (
        P(None, "space", None),
        P(None, "space", None),
        P(),
        P(),
        P("segment", None, None),
        P(),
        P(),
        P("segment", None, None),
        P("segment", None),
        P("space", None, None),
        P("space", None, None),
    )
    out_specs = P(None, "space", "segment")
    return jax.shard_map(
        per_device, mesh=mesh, in_specs=in_specs, out_specs=out_specs, check_vma=False
    )
```

time: 414 us -> 68.9 us (0.17)
  the two profiles are of different devices: /device:TPU:122 before, /device:TPU:129 now
where the time goes in v1:
time: 68.9 us; the launch traced here: 68.7 us
  Pallas kernels  65.6 us (95%)
  local copies, waits for them, and re-layouts  3.1 us (4%)
    pallas_call x1, Pallas kernels, per_device(): pl.pallas_call(functools.partial(kernel, lax.axis_size('space')), out_sha...  65.6 us
    unnamed x1, local copies, waits for them, and re-layouts  1.59 us
    pallas_call x1, local copies, waits for them, and re-layouts, per_device(): pl.pallas_call(functools.partial(kernel, lax.axis_size('space')), out_sha...  1.52 us

profile of v1, /device:TPU:129, one launch (start us, length us, event | category | flops | bytes accessed | tf_op | source)
XLA Modules:
  0.0 68.7 jit_solution(12525548642547016338)
XLA Ops:
  0.0 1.6 %copy.12.patch_out = bf16[1024,16]{1,0:T(8,128)(2,1)} copy(bf16[1024,16]{0,1:T(8,128)(2,1)} %param.17) | data formatting | bytes 65536 | tf_op args[6]
  1.6 65.6 %shard_map.109 = f32[2,64,16]{2,1,0:T(8,128)} custom-call(f32[2,64,64]{2,1,0:T(8,128)} %frames.1, f32[2,64,64]{2,1,0:T(8,128)} %noise.1, s32[2]{0:T(128)} %steps.1, f32[128]{0:T(128)} %freqs.1, bf16[1,256,1024]{2,1,0:T(8,128)(2,1)} %cond.1, f32[16,1024]{1,0:T(8,128)} %patch_in.1, bf16[1024,16]{1,0:T(8,128)(2,1)} %copy.12.patch_out, ...), custom_call_target="tpu_custom_call" | custom-call | tf_op jit(solution)/shard_map/pallas_call | solution.py:608
  67.2 1.5 %copy.13 = f32[2,64,16]{1,2,0:T(8,128)} copy(f32[2,64,16]{2,1,0:T(8,128)} %shard_map.109) | data formatting | bytes 16384 | tf_op jit(solution)/shard_map/pallas_call | solution.py:608

commit v2 on v1

v2 whole, which is shorter than its diff:
```python
import functools
import math

import jax
import jax.numpy as jnp
from jax import lax
from jax.experimental import pallas as pl
from jax.experimental.pallas import tpu as pltpu
from jax.sharding import PartitionSpec as P

STEPS = 1000
MB = 2
D = 1024
FI = 512
CI = 1536
G = 256
OWN = 256
FINE = 384
COWN = 64
COARSE = 128
EPS = 1e-06

LOG_LOW = math.log(0.002)
LOG_HIGH = math.log(80.0)
LOG2E = 1.0 / math.log(2.0)

F32 = jnp.float32
BF16 = jnp.bfloat16
NT = (((1,), (1,)), ((), ()))
NN = (((1,), (0,)), ((), ()))

CHUNK = 256
CHUNKS = 24


def dot_nt(a, b):
    return lax.dot_general(a, b, NT, preferred_element_type=F32)


def dot_nn(a, b):
    return lax.dot_general(a, b, NN, preferred_element_type=F32)


def iota(shape, dim):
    return lax.broadcasted_iota(jnp.int32, shape, dim)


def split3(value):
    hi = value.astype(BF16)
    rest = value - hi.astype(F32)
    mid = rest.astype(BF16)
    return hi, mid, (rest - mid.astype(F32)).astype(BF16)


def kernel(
    n_space,
    frames_hbm, noise_hbm, steps, freqs_hbm, cond_hbm, patch_in_hbm, patch_out_hbm, w_hbm, scales, fine_links,
    coarse_links,
    out,
    w, wt, frames, noise, freqs, cond, patch_in, patch_out, xs, x, nrm, halo, q_s, k_s, v_s, mix, grp, skip, cin, cout,
    w3, pox, gains, qscale, links, fmask, cmask, pixout, pixin, placed,
    w_sem, in_sem, halo_s, halo_r, link_s, link_r, c_s, c_r, skip_s, skip_r, fwd_s, fwd_r, pix_s, pix_r,
):
    s = lax.axis_index("segment")
    p = lax.axis_index("space")
    b = p + (s // 2) * (1 - 2 * (p % 2))
    has_up = b > 0
    has_down = b < n_space - 1

    def place(seg, block):
        return block + (seg // 2) * (1 - 2 * (block % 2))

    def remote(src, dst, ssem, rsem, seg, block):
        return pltpu.make_async_remote_copy(
            src_ref=src, dst_ref=dst, send_sem=ssem, recv_sem=rsem,
            device_id=(seg, place(seg, block)), device_id_type=pl.DeviceIdType.MESH,
        )

    def arrived(dst, rsem):
        pltpu.make_async_remote_copy(
            src_ref=dst, dst_ref=dst, send_sem=rsem, recv_sem=rsem,
            device_id=(s, p), device_id_type=pl.DeviceIdType.MESH,
        ).wait_recv()

    def weight_copy(i):
        rows = pl.ds(i * CHUNK, CHUNK)
        return pltpu.make_async_copy(w_hbm.at[0, rows, :], w.at[rows, :], w_sem.at[i])

    freq_copy = pltpu.make_async_copy(freqs_hbm, freqs, in_sem.at[0])
    cond_copy = pltpu.make_async_copy(cond_hbm, cond, in_sem.at[1])
    frame_copy = pltpu.make_async_copy(frames_hbm, frames, in_sem.at[2])
    noise_copy = pltpu.make_async_copy(noise_hbm, noise, in_sem.at[3])
    patch_in_copy = pltpu.make_async_copy(patch_in_hbm, patch_in, in_sem.at[4])
    patch_out_copy = pltpu.make_async_copy(patch_out_hbm, patch_out, in_sem.at[5])

    barrier = pltpu.get_barrier_semaphore()

    def greet(seg, space):
        pl.semaphore_signal(barrier, inc=1, device_id=(seg, space), device_id_type=pl.DeviceIdType.MESH)

    @pl.when((s == 0) | (s == 3))
    def _():
        @pl.when(has_up)
        def _():
            greet(s, place(s, b - 1))

        @pl.when(has_down)
        def _():
            greet(s, place(s, b + 1))

    @pl.when(s == 0)
    def _():
        frame_copy.start()
        noise_copy.start()
        patch_in_copy.start()

    freq_copy.start()
    cond_copy.start()
    for i in range(CHUNKS):
        weight_copy(i).start()

    greet(3, place(3, p))

    @pl.when(s > 0)
    def _():
        greet(s - 1, place(s - 1, b))

        @pl.when(has_up)
        def _():
            greet(s - 1, place(s - 1, b - 1))

        @pl.when(has_down)
        def _():
            greet(s - 1, place(s - 1, b + 1))

    @pl.when(s == 3)
    def _():
        greet(0, b)
        patch_out_copy.start()

    def level_row(m):
        step = jnp.full((1, 128), steps[m], jnp.int32).astype(F32)
        return jnp.exp(LOG_LOW + step / (STEPS - 1) * (LOG_HIGH - LOG_LOW))

    lane = iota((1, G), 1) // 64
    for g in range(6):
        four = [scales[0, 4 * g + h] for h in range(4)]
        row = jnp.where(lane == 0, four[0], jnp.where(lane == 1, four[1], jnp.where(lane == 2, four[2], four[3])))
        qscale[g : g + 1, :] = row * (LOG2E / 64.0)

    head_mean = jnp.where(iota((G, G), 0) // 64 == iota((G, G), 1) // 64, 1.0 / 64.0, 0.0).astype(BF16)
    ones = jnp.ones((G, 128), BF16)

    def make_gains():
        rows = []
        for m in range(MB):
            phases = 2.0 * math.pi * (jnp.log(level_row(m)) / 4.0) * freqs[...].reshape(1, 128)
            rows.append(jnp.concatenate([jnp.cos(phases), jnp.sin(phases)], axis=1))
        features = jnp.concatenate(rows + [jnp.zeros((6, 256), F32)], axis=0)
        hi, mid, low = split3(features)
        gains[...] = 1.0 + (dot_nn(hi, cond[0]) + dot_nn(mid, cond[0]) + dot_nn(low, cond[0]))

    def make_fine_mask():
        query = iota((128, 256), 0)
        key = iota((128, 256), 1)
        row_gap = key // 16 - 4 - query // 16
        query_col = 2 * (query % 8) + (query // 8) % 2
        key_col = 2 * (key % 8) + (key // 8) % 2
        col_gap = key_col - query_col
        near = (row_gap <= 3) & (row_gap >= -3) & (col_gap <= 3) & (col_gap >= -3)
        for t in range(2):
            left = jnp.broadcast_to(links[2 * t : 2 * t + 1, :], (128, 256))
            right = jnp.broadcast_to(links[2 * t + 1 : 2 * t + 2, :], (128, 256))
            value = jnp.where(query_col < 8, left, right)
            fmask[t] = jnp.where(near, value, 0.0).astype(BF16)

    def make_coarse_mask():
        query = iota((64, 128), 0)
        key = iota((64, 128), 1)
        row_gap = key // 8 - 4 - query // 8
        col_gap = key % 8 - query % 8
        near = (row_gap <= 3) & (row_gap >= -3) & (col_gap <= 3) & (col_gap >= -3)
        value = jnp.broadcast_to(links[0:1, 0:128], (64, 128))
        cmask[...] = jnp.where(near, value, 0.0).astype(BF16)

    def make_fine_links():
        key = iota((1, 256), 1)
        key_row = key // 16
        key_tile = (key % 8) // 4
        for t in range(2):
            for c in range(2):
                row = jnp.zeros((1, 256), F32)
                for dy in range(3):
                    in_row = (key_row >= (0, 4, 12)[dy]) & (key_row < (4, 12, 16)[dy])
                    for kc in range(2):
                        link = fine_links[t, c, 3 * dy + kc - c + 1].astype(F32)
                        row = jnp.where(in_row & (key_tile == kc), link, row)
                links[2 * t + c : 2 * t + c + 1, :] = row

    def make_coarse_links():
        key_row = iota((1, 256), 1) // 8
        row = jnp.zeros((1, 256), F32)
        for dy in range(3):
            in_row = (key_row >= (0, 4, 12)[dy]) & (key_row < (4, 12, 16)[dy])
            row = jnp.where(in_row, coarse_links[0, 0, 3 * dy + 1].astype(F32), row)
        links[0:1, :] = row

    def halo_up():
        return remote(xs.at[:, pl.ds(16, 16), :], xs.at[:, pl.ds(80, 16), :], halo_s.at[0], halo_r.at[1], 0, b - 1)

    def halo_down():
        return remote(xs.at[:, pl.ds(64, 16), :], xs.at[:, pl.ds(0, 16), :], halo_s.at[1], halo_r.at[0], 0, b + 1)

    def link_copy(seg):
        return remote(links, links, link_s, link_r, seg, b)

    edges = has_up.astype(jnp.int32) + has_down.astype(jnp.int32)

    def scale_pixels():
        for m in range(MB):
            level = level_row(m)[:, 0:64]
            scaled = (frames[m] + level * noise[m]) * lax.rsqrt(level * level + 0.25)
            xs[m, 16:80, :] = jnp.concatenate([scaled, jnp.zeros((64, 64), F32)], axis=1)

        @pl.when(b == 0)
        def _():
            xs[:, 0:16, :] = jnp.zeros((MB, 16, 128), F32)

        @pl.when(b == n_space - 1)
        def _():
            xs[:, 80:96, :] = jnp.zeros((MB, 16, 128), F32)

    def make_embedding():
        entry = iota((256, 16), 0)
        pick = (iota((256, 16), 1) == 4 * (entry // 64) + entry % 4).astype(BF16)
        hi, low, _ = split3(patch_in[...])
        wide = dot_nn(pick, hi).astype(BF16)
        w3[0:256, :] = wide
        w3[256:512, :] = dot_nn(pick, low).astype(BF16)
        w3[512:768, :] = wide

    def transpose_weights(first, count):
        eye = (iota((G, G), 0) == iota((G, G), 1)).astype(BF16)

        def tile(i, carry):
            weight_copy(first + i).wait()
            row = pl.multiple_of((first + i) * G, G)
            col = pl.multiple_of(i * G, G)
            for k in range(D // G):
                block = dot_nt(eye, w[pl.ds(row, G), k * G : (k + 1) * G])
                wt[k * G : (k + 1) * G, pl.ds(col, G)] = block.astype(BF16)
            return carry

        lax.fori_loop(0, count, tile, 0)

    def normed(value, m):
        scale = lax.rsqrt(jnp.mean(value * value, axis=-1, keepdims=True) + EPS)
        return (value * scale * gains[pl.ds(m, 1), :]).astype(BF16)

    def embed(rows4):
        flat = jnp.concatenate(
            [rows4[0] + pltpu.roll(rows4[1], 64, 1), rows4[2] + pltpu.roll(rows4[3], 64, 1)], axis=1
        )
        hi, low, _ = split3(flat)
        token = iota((16, 256), 0)
        col = iota((16, 256), 1)
        own = ((col % 64) // 4 == 2 * (token % 8) + token // 8).astype(F32)
        count = flat.shape[0]

        def spread(piece):
            wide = jnp.broadcast_to(piece.astype(F32)[:, None, :], (count, 16, 256)) * own[None]
            return wide.reshape(count * 16, 256).astype(BF16)

        first = spread(hi)
        return dot_nn(jnp.concatenate([first, first, spread(low)], axis=1), w3[...])

    def run_jobs(jobs):
        def finish(block, part, g, put):
            if part < 2:
                power = dot_nn((block * block).astype(BF16), head_mean)
                block = block * lax.rsqrt(power + EPS)
            if part == 0:
                block = block * qscale[g : g + 1, :]
            put(block.astype(BF16))

        pending = []
        for make, part, g, put in jobs:
            pending.append((make(), part, g, put))
            if len(pending) > 2:
                finish(*pending.pop(0))
        for job in pending:
            finish(*job)

    def fine_jobs(source, first, count, parts, put):
        jobs = []
        for part in parts:
            for g in range(FI // G):
                at = part * FI + g * G
                lo, n = (first, count) if part == 0 else (0, source.shape[0])
                jobs.append(
                    (
                        lambda at=at, lo=lo, n=n: dot_nt(source[lo : lo + n, :], w[at : at + G, :]),
                        part, g, functools.partial(put, part, g),
                    )
                )
        return jobs

    def embed_own():
        for m in range(MB):
            own = embed([xs[m, pl.ds(16 + a, 16, stride=4), :] for a in range(4)])
            x[m, 2:10] = own.reshape(8, 2, 2, 8, D)
            nrm[m * OWN : (m + 1) * OWN, :] = normed(own, m)

    def project_own():
        def put(part, g, block):
            for m in range(MB):
                rows = block[m * OWN : (m + 1) * OWN]
                if part == 0:
                    q_s[2 * m + g, :, :] = rows
                else:
                    (k_s if part == 1 else v_s)[2 * m + g, 64:320, :] = rows

        run_jobs(fine_jobs(nrm, 0, 2 * OWN, (0, 1, 2), put))

    def project_halo():
        for m in range(MB):
            rows4 = [
                jnp.concatenate(
                    [xs[m, pl.ds(a, 4, stride=4), :], xs[m, pl.ds(80 + a, 4, stride=4), :]], axis=0
                )
                for a in range(4)
            ]
            halo[m * 128 : (m + 1) * 128, :] = normed(embed(rows4), m)

        def put(part, g, block):
            dst = k_s if part == 1 else v_s
            for m in range(MB):
                dst[2 * m + g, 0:64, :] = block[m * 128 : m * 128 + 64]
                dst[2 * m + g, 320:384, :] = block[m * 128 + 64 : m * 128 + 128]

        run_jobs(fine_jobs(halo, 0, 256, (1, 2), put))

    def widen(m):
        coarse = cin[m, 16:112, :]
        for a in range(2):
            for c in range(2):
                at = (2 * a + c) * D
                x[m, :, a, c] = dot_nn(coarse, wt[:, at : at + D]).reshape(12, 8, D)
        x[m] += skip[m].astype(F32).reshape(12, 2, 2, 8, D)

    def project_fine(m):
        nrm[0:FINE, :] = normed(x[m].reshape(FINE, D), m)

        def put(part, g, block):
            (q_s, k_s, v_s)[part][2 * m + g, :, :] = block

        run_jobs(fine_jobs(nrm.at[0:FINE], 64, OWN, (0, 1, 2), put))

    def attend(queries, keys, values, mask, count):
        head = iota((count, G), 1) // 64
        stacked = jnp.concatenate(
            [jnp.where(head == h, queries, jnp.zeros_like(queries)) for h in range(4)], axis=0
        )
        expo = jnp.exp2(dot_nt(stacked, keys)).astype(BF16)
        expo = expo * jnp.concatenate([mask] * 4, axis=0)
        mixed = dot_nn(expo, values)
        total = dot_nn(expo, ones[0 : keys.shape[0], :])
        part = [mixed[h * count : (h + 1) * count] for h in range(4)]
        sums = [total[h * count : (h + 1) * count] for h in range(4)]
        first = head[:, 0:128] == 0
        number = jnp.concatenate(
            [
                jnp.where(first, part[0][:, 0:128], part[1][:, 0:128]),
                jnp.where(first, part[2][:, 128:256], part[3][:, 128:256]),
            ],
            axis=1,
        )
        weight = jnp.concatenate(
            [jnp.where(first, sums[0], sums[1]), jnp.where(first, sums[2], sums[3])], axis=1
        )
        return (number / weight).astype(BF16)

    def mix_fine(m):
        for t in range(2):
            for g in range(2):
                mix[128 * t : 128 * t + 128, g * G : (g + 1) * G] = attend(
                    q_s[2 * m + g, 128 * t : 128 * t + 128, :],
                    k_s[2 * m + g, 128 * t : 128 * t + 256, :],
                    v_s[2 * m + g, 128 * t : 128 * t + 256, :],
                    fmask[t],
                    128,
                )
        update = dot_nn(mix[:, 0:FI], w[3 * FI : 4 * FI, :])
        x[m, 2:10] += update.reshape(8, 2, 2, 8, D)

    def coarse_jobs(first, count, parts):
        jobs = []
        for part in parts:
            for g in range(CI // G):
                at = part * CI + g * G

                def put(block, part=part, g=g):
                    (q_s, k_s, v_s)[part][g, 0:count, :] = block

                jobs.append(
                    (lambda at=at: dot_nn(nrm[first : first + count, :], wt[:, at : at + G]), part, g, put)
                )
        return jobs

    def coarse_queries(m):
        nrm[32:96, :] = normed(cin[m, 32:96, :].astype(F32), m)
        run_jobs(coarse_jobs(32, COWN, (0,)))

    def coarse_rest(m):
        nrm[0:32, :] = normed(cin[m, 0:32, :].astype(F32), m)
        nrm[96:128, :] = normed(cin[m, 96:128, :].astype(F32), m)
        run_jobs(coarse_jobs(0, COARSE, (1, 2)))
        for g in range(6):
            mix[0:COWN, g * G : (g + 1) * G] = attend(
                q_s[g, 0:COWN, :], k_s[g, 0:COARSE, :], v_s[g, 0:COARSE, :], cmask[...], COWN
            )
        update = dot_nn(mix[0:COWN, :], w[3 * CI : 4 * CI, :])
        cout[m] = (cin[m, 32:96, :].astype(F32) + update).astype(BF16)

    def merge(m):
        own = x[m, 2:10]
        skip[m, 64:320, :] = own.reshape(OWN, D).astype(BF16)
        for a in range(2):
            for c in range(2):
                at = (2 * a + c) * D
                grp[:, at : at + D] = own[:, a, c].reshape(COWN, D).astype(BF16)
        cout[m] = dot_nn(grp[...], w[4 * FI :, :]).astype(BF16)

    def head(m):
        top = x[m, 2:10].reshape(OWN, D)
        scale = lax.rsqrt(jnp.mean(top * top, axis=-1, keepdims=True) + EPS)
        pixels = dot_nn((top * scale).astype(BF16), pox[...])
        token = iota((16, 256), 0)
        col = iota((16, 256), 1)
        own = 2 * (token % 8) + token // 8 == 4 * (col // 64) + (col // 4) % 4
        spread = jnp.where(own[None], pixels.reshape(16, 16, 256), 0.0)
        total = jnp.sum(spread, axis=1)
        pixout[m, 0] = total[:, 0:128]
        pixout[m, 1] = total[:, 128:256]

    def coarse_own(m, seg):
        return remote(cout.at[m], cin.at[m, pl.ds(32, 64), :], c_s.at[m, 0], c_r.at[m, 0], seg + 1, b)

    def coarse_up(m, seg, rows):
        return remote(
            cout.at[m, pl.ds(0, rows), :], cin.at[m, pl.ds(96, rows), :], c_s.at[m, 1], c_r.at[m, 2], seg + 1, b - 1
        )

    def coarse_down(m, seg, rows):
        return remote(
            cout.at[m, pl.ds(64 - rows, rows), :], cin.at[m, pl.ds(32 - rows, rows), :],
            c_s.at[m, 2], c_r.at[m, 1], seg + 1, b + 1,
        )

    def send_coarse(m, seg, rows, act):
        @pl.when(has_up)
        def _():
            act(coarse_up(m, seg, rows))

        @pl.when(has_down)
        def _():
            act(coarse_down(m, seg, rows))

        act(coarse_own(m, seg))

    def take_own(m):
        arrived(cin.at[m, pl.ds(32, 64), :], c_r.at[m, 0])

    def take_halos(m, rows):
        @pl.when(has_up)
        def _():
            arrived(cin.at[m, pl.ds(32 - rows, rows), :], c_r.at[m, 1])

        @pl.when(has_down)
        def _():
            arrived(cin.at[m, pl.ds(96, rows), :], c_r.at[m, 2])

    def skip_copy(m):
        return remote(
            skip.at[m, pl.ds(64, OWN), :], skip.at[m, pl.ds(64, OWN), :], skip_s.at[m], skip_r.at[m], 3, b
        )

    def skip_up(m):
        return remote(
            skip.at[m, pl.ds(64, 64), :], skip.at[m, pl.ds(320, 64), :], fwd_s.at[m, 0], fwd_r.at[m, 1], 3, b - 1
        )

    def skip_down(m):
        return remote(
            skip.at[m, pl.ds(256, 64), :], skip.at[m, pl.ds(0, 64), :], fwd_s.at[m, 1], fwd_r.at[m, 0], 3, b + 1
        )

    def forward_skip(m, act):
        @pl.when(has_up)
        def _():
            act(skip_up(m))

        @pl.when(has_down)
        def _():
            act(skip_down(m))

    def pixel_copy(m, seg):
        return pltpu.make_async_remote_copy(
            src_ref=pixout.at[m, seg // 2], dst_ref=pixin.at[m], send_sem=pix_s.at[m, seg], recv_sem=pix_r.at[m],
            device_id=(seg, b), device_id_type=pl.DeviceIdType.MESH,
        )

    def start(copy):
        copy.start()

    def sent(copy):
        copy.wait_send()

    freq_copy.wait()
    cond_copy.wait()
    make_gains()

    @pl.when(s == 0)
    def _():
        frame_copy.wait()
        noise_copy.wait()
        scale_pixels()
        patch_in_copy.wait()
        make_embedding()
        make_fine_links()
        make_fine_mask()
        embed_own()
        pl.semaphore_wait(barrier, 2 + 2 * edges)

        @pl.when(has_up)
        def _():
            halo_up().start()

        @pl.when(has_down)
        def _():
            halo_down().start()

        link_copy(3).start()
        for i in range(3 * FI // CHUNK):
            weight_copy(i).wait()
        project_own()

        @pl.when(has_up)
        def _():
            arrived(xs.at[:, pl.ds(0, 16), :], halo_r.at[0])

        @pl.when(has_down)
        def _():
            arrived(xs.at[:, pl.ds(80, 16), :], halo_r.at[1])

        project_halo()
        for i in range(3 * FI // CHUNK, CHUNKS):
            weight_copy(i).wait()

    @pl.when((s == 1) | (s == 2))
    def _():
        @pl.when(b == 0)
        def _():
            cin[:, 0:32, :] = jnp.zeros((MB, 32, D), BF16)

        @pl.when(b == n_space - 1)
        def _():
            cin[:, 96:128, :] = jnp.zeros((MB, 32, D), BF16)

        transpose_weights(0, 3 * CI // G)
        for i in range(3 * CI // CHUNK, CHUNKS):
            weight_copy(i).wait()
        pl.semaphore_wait(barrier, 1 + edges)

    @pl.when(s == 1)
    def _():
        make_coarse_links()
        link_copy(2).start()
        make_coarse_mask()

    @pl.when(s == 2)
    def _():
        arrived(links, link_r)
        make_coarse_mask()

    @pl.when(s == 3)
    def _():
        @pl.when(b == 0)
        def _():
            cin[:, 16:32, :] = jnp.zeros((MB, 16, D), BF16)
            skip[:, 0:64, :] = jnp.zeros((MB, 64, D), BF16)

        @pl.when(b == n_space - 1)
        def _():
            cin[:, 96:112, :] = jnp.zeros((MB, 16, D), BF16)
            skip[:, 320:384, :] = jnp.zeros((MB, 64, D), BF16)

        for i in range(4 * FI // CHUNK):
            weight_copy(i).wait()
        transpose_weights(4 * FI // G, 4 * D // G)
        patch_out_copy.wait()
        entry = iota((16, 256), 0)
        col = iota((16, 256), 1)
        pick = (entry == 4 * ((col // 16) % 4) + col % 4).astype(BF16)
        pox[...] = lax.dot_general(
            patch_out[...], pick, (((0,), (0,)), ((), ())), preferred_element_type=F32
        ).astype(BF16)
        pl.semaphore_wait(barrier, 4 + edges)
        arrived(links, link_r)
        make_fine_mask()
        arrived(skip.at[0, pl.ds(64, OWN), :], skip_r.at[0])
        forward_skip(0, start)

    def one_batch(m, carry):
        @pl.when(s == 3)
        def _():
            take_own(m)
            take_halos(m, 16)

            @pl.when(has_up)
            def _():
                arrived(skip.at[m, pl.ds(0, 64), :], fwd_r.at[m, 0])

            @pl.when(has_down)
            def _():
                arrived(skip.at[m, pl.ds(320, 64), :], fwd_r.at[m, 1])

            widen(m)

            @pl.when(m == 0)
            def _():
                arrived(skip.at[1, pl.ds(64, OWN), :], skip_r.at[1])
                forward_skip(1, start)

            project_fine(m)

        @pl.when((s == 0) | (s == 3))
        def _():
            mix_fine(m)

        @pl.when(s == 0)
        def _():
            merge(m)
            send_coarse(m, 0, 32, start)
            skip_copy(m).start()

        @pl.when(s == 3)
        def _():
            head(m)
            for seg in range(4):
                pixel_copy(m, seg).start()

        @pl.when((s == 1) | (s == 2))
        def _():
            take_own(m)
            coarse_queries(m)
            take_halos(m, 32)
            coarse_rest(m)

        @pl.when(s == 1)
        def _():
            send_coarse(m, 1, 32, start)

        @pl.when(s == 2)
        def _():
            send_coarse(m, 2, 16, start)

        return carry

    lax.fori_loop(0, MB, one_batch, 0)

    for m in range(MB):
        arrived(pixin.at[m], pix_r.at[m])
        pixels = pixin[m]
        pixels = jnp.where(s % 2 == 1, pltpu.roll(pixels, 64, 1), pixels)
        for a in range(4):
            placed[pl.ds(a, 16, stride=4), :] = pltpu.roll(pixels, (128 - 16 * a) % 128, 1)
        out[m] = placed[...].T[0:16, :]

    @pl.when(s == 0)
    def _():
        @pl.when(has_up)
        def _():
            halo_up().wait_send()

        @pl.when(has_down)
        def _():
            halo_down().wait_send()

        link_copy(3).wait_send()
        for m in range(MB):
            send_coarse(m, 0, 32, sent)
            skip_copy(m).wait_send()

    @pl.when(s == 1)
    def _():
        link_copy(2).wait_send()
        for m in range(MB):
            send_coarse(m, 1, 32, sent)

    @pl.when(s == 2)
    def _():
        for m in range(MB):
            send_coarse(m, 2, 16, sent)

    @pl.when(s == 3)
    def _():
        for m in range(MB):
            forward_skip(m, sent)
            for seg in range(4):
                pixel_copy(m, seg).wait_send()


def per_device(
    clean_frames, noise, noise_steps, noise_freqs, cond_weights, patch_in, patch_out, section_weights, head_scales,
    fine_links, coarse_links,
):
    vmem = pl.BlockSpec(memory_space=pltpu.VMEM)
    smem = pl.BlockSpec(memory_space=pltpu.SMEM)
    hbm = pl.BlockSpec(memory_space=pl.ANY)
    dma = pltpu.SemaphoreType.DMA
    placed = pl.pallas_call(
        functools.partial(kernel, lax.axis_size("space")),
        out_shape=jax.ShapeDtypeStruct((MB, 16, 64), F32),
        in_specs=[hbm, hbm, smem, hbm, hbm, hbm, hbm, hbm, smem, smem, smem],
        out_specs=vmem,
        scratch_shapes=[
            pltpu.VMEM((6144, D), BF16),
            pltpu.VMEM((D, 3 * CI), BF16),
            pltpu.VMEM((MB, 64, 64), F32),
            pltpu.VMEM((MB, 64, 64), F32),
            pltpu.VMEM((128,), F32),
            pltpu.VMEM((1, 256, D), BF16),
            pltpu.VMEM((16, D), F32),
            pltpu.VMEM((16, D), BF16),
            pltpu.VMEM((MB, 96, 128), F32),
            pltpu.VMEM((MB, 12, 2, 2, 8, D), F32),
            pltpu.VMEM((2 * OWN, D), BF16),
            pltpu.VMEM((256, D), BF16),
            pltpu.VMEM((6, OWN, G), BF16),
            pltpu.VMEM((6, FINE, G), BF16),
            pltpu.VMEM((6, FINE, G), BF16),
            pltpu.VMEM((OWN, CI), BF16),
            pltpu.VMEM((COWN, 4 * D), BF16),
            pltpu.VMEM((MB, FINE, D), BF16),
            pltpu.VMEM((MB, COARSE, D), BF16),
            pltpu.VMEM((MB, COWN, D), BF16),
            pltpu.VMEM((768, D), BF16),
            pltpu.VMEM((D, 256), BF16),
            pltpu.VMEM((8, D), F32),
            pltpu.VMEM((8, G), F32),
            pltpu.VMEM((8, 256), F32),
            pltpu.VMEM((2, 128, 256), BF16),
            pltpu.VMEM((64, 128), BF16),
            pltpu.VMEM((MB, 2, 16, 128), F32),
            pltpu.VMEM((MB, 16, 128), F32),
            pltpu.VMEM((64, 128), F32),
            dma((CHUNKS,)),
            dma((6,)),
            dma((2,)), dma((2,)),
            dma(()), dma(()),
            dma((MB, 3)), dma((MB, 3)),
            dma((MB,)), dma((MB,)),
            dma((MB, 2)), dma((MB, 2)),
            dma((MB, 4)), dma((MB,)),
        ],
        compiler_params=pltpu.CompilerParams(
            collective_id=0, has_side_effects=True, vmem_limit_bytes=58 << 20
        ),
    )(
        clean_frames, noise, noise_steps, noise_freqs, cond_weights, patch_in, patch_out.T, section_weights,
        head_scales, fine_links, coarse_links,
    )
    return placed.transpose(0, 2, 1)


def solution(mesh):
    in_specs = (
        P(None, "space", None),
        P(None, "space", None),
        P(),
        P(),
        P("segment", None, None),
        P(),
        P(),
        P("segment", None, None),
        P("segment", None),
        P("space", None, None),
        P("space", None, None),
    )
    out_specs = P(None, "space", "segment")
    return jax.shard_map(
        per_device, mesh=mesh, in_specs=in_specs, out_specs=out_specs, check_vma=False
    )
```

time: 68.9 us -> 58.5 us (0.85)
  Pallas kernels: 65.6 us -> 57 us
  local copies, waits for them, and re-layouts: 3.1 us -> 1.32 us
    pallas_call x1, Pallas kernels: 65.6 us -> 57 us  [per_device(): pl.pallas_call(functools.partial(kernel, lax.axis_size('space')), out_sha...]
    pallas_call x1 -> x0, local copies, waits for them, and re-layouts: 1.52 us -> none  [per_device(): pl.pallas_call(functools.partial(kernel, lax.axis_size('space')), out_sha...]
where the time goes in v2:
time: 58.5 us; the launch traced here: 58.4 us
  Pallas kernels  57 us (97%)
  local copies, waits for them, and re-layouts  1.32 us (2%)
    pallas_call x1, Pallas kernels, per_device(): pl.pallas_call(functools.partial(kernel, lax.axis_size('space')), out_sha...  57 us
    unnamed x1, local copies, waits for them, and re-layouts  1.32 us

profile of v2, /device:TPU:129, one launch (start us, length us, event | category | flops | bytes accessed | tf_op | source)
XLA Modules:
  0.0 58.4 jit_solution(15725098961519343467)
XLA Ops:
  0.0 57.0 %shard_map.109 = f32[2,16,64]{2,1,0:T(8,128)} custom-call(f32[2,64,64]{2,1,0:T(8,128)} %frames_hbm.1, f32[2,64,64]{2,1,0:T(8,128)} %noise_hbm.1, s32[2]{0:T(128)} %steps.1, f32[128]{0:T(128)} %freqs_hbm.1, bf16[1,256,1024]{2,1,0:T(8,128)(2,1)} %cond_hbm.1, f32[16,1024]{1,0:T(8,128)} %patch_in_hbm.1, bf16[16,1024]{1,0:T(8,128)(2,1)} %bitcast.3, ...), custom_call_target="tpu_custom_call" | custom-call | tf_op jit(solution)/shard_map/pallas_call | solution.py:722
  57.0 1.3 %copy.13 = f32[2,64,16]{1,2,0:T(8,128)} copy(f32[2,64,16]{1,2,0:T(8,128)} %bitcast.2) | data formatting | bytes 16384

commit v3 on v2

--- a/solution.py
+++ b/solution.py
@@ -57,9 +57,10 @@
     frames_hbm, noise_hbm, steps, freqs_hbm, cond_hbm, patch_in_hbm, patch_out_hbm, w_hbm, scales, fine_links,
     coarse_links,
     out,
-    w, wt, frames, noise, freqs, cond, patch_in, patch_out, xs, x, nrm, halo, q_s, k_s, v_s, mix, grp, skip, cin, cout,
-    w3, pox, gains, qscale, links, fmask, cmask, pixout, pixin, placed,
-    w_sem, in_sem, halo_s, halo_r, link_s, link_r, c_s, c_r, skip_s, skip_r, fwd_s, fwd_r, pix_s, pix_r,
+    w, wt, frames, noise, freqs, cond, patch_in, patch_out, xs, x, nrm, halo, q_s, k_s, v_s, mix, mixed, grp, wo, cin, cout,
+    edge_out, edge_in, w3, pox, gains, qscale, links, fmask, cmask, pixout, pixin, placed,
+    w_sem, in_sem, halo_s, halo_r, link_s, link_r, c_s, c_r, xs_s, xs_r, wo_s, wo_r, mix_s, mix_r, fwd_s,
+    fwd_r, pix_s, pix_r,
 ):
     s = lax.axis_index("segment")
     p = lax.axis_index("space")
@@ -112,6 +113,9 @@
     def _():
         frame_copy.start()
         noise_copy.start()
+
+    @pl.when((s == 0) | (s == 3))
+    def _():
         patch_in_copy.start()
 
     freq_copy.start()
@@ -149,7 +153,6 @@
         qscale[g : g + 1, :] = row * (LOG2E / 64.0)
 
     head_mean = jnp.where(iota((G, G), 0) // 64 == iota((G, G), 1) // 64, 1.0 / 64.0, 0.0).astype(BF16)
-    ones = jnp.ones((G, 128), BF16)
 
     def make_gains():
         rows = []
@@ -305,48 +308,49 @@
                 )
         return jobs
 
-    def embed_own():
-        for m in range(MB):
-            own = embed([xs[m, pl.ds(16 + a, 16, stride=4), :] for a in range(4)])
-            x[m, 2:10] = own.reshape(8, 2, 2, 8, D)
-            nrm[m * OWN : (m + 1) * OWN, :] = normed(own, m)
-
-    def project_own():
+    def embed_own(m):
+        own = embed([xs[m, pl.ds(16 + a, 16, stride=4), :] for a in range(4)])
+        x[m, 2:10] = own.reshape(8, 2, 2, 8, D)
+        nrm[m * OWN : (m + 1) * OWN, :] = normed(own, m)
+
+    def project_own(m):
         def put(part, g, block):
-            for m in range(MB):
-                rows = block[m * OWN : (m + 1) * OWN]
-                if part == 0:
-                    q_s[2 * m + g, :, :] = rows
-                else:
-                    (k_s if part == 1 else v_s)[2 * m + g, 64:320, :] = rows
-
-        run_jobs(fine_jobs(nrm, 0, 2 * OWN, (0, 1, 2), put))
-
-    def project_halo():
-        for m in range(MB):
-            rows4 = [
-                jnp.concatenate(
-                    [xs[m, pl.ds(a, 4, stride=4), :], xs[m, pl.ds(80 + a, 4, stride=4), :]], axis=0
-                )
-                for a in range(4)
-            ]
-            halo[m * 128 : (m + 1) * 128, :] = normed(embed(rows4), m)
+            if part == 0:
+                q_s[2 * m + g, :, :] = block
+            else:
+                (k_s if part == 1 else v_s)[2 * m + g, 64:320, :] = block
+
+        own = nrm.at[pl.ds(pl.multiple_of(m * OWN, OWN), OWN), :]
+        run_jobs(fine_jobs(own, 0, OWN, (0, 1, 2), put))
+
+    def project_halo(m):
+        rows4 = [
+            jnp.concatenate([xs[m, pl.ds(a, 4, stride=4), :], xs[m, pl.ds(80 + a, 4, stride=4), :]], axis=0)
+            for a in range(4)
+        ]
+        halo[...] = normed(embed(rows4), m)
 
         def put(part, g, block):
             dst = k_s if part == 1 else v_s
-            for m in range(MB):
-                dst[2 * m + g, 0:64, :] = block[m * 128 : m * 128 + 64]
-                dst[2 * m + g, 320:384, :] = block[m * 128 + 64 : m * 128 + 128]
-
-        run_jobs(fine_jobs(halo, 0, 256, (1, 2), put))
+            dst[2 * m + g, 0:64, :] = block[0:64]
+            dst[2 * m + g, 320:384, :] = block[64:128]
+
+        run_jobs(fine_jobs(halo, 0, 128, (1, 2), put))
 
     def widen(m):
         coarse = cin[m, 16:112, :]
         for a in range(2):
             for c in range(2):
                 at = (2 * a + c) * D
-                x[m, :, a, c] = dot_nn(coarse, wt[:, at : at + D]).reshape(12, 8, D)
-        x[m] += skip[m].astype(F32).reshape(12, 2, 2, 8, D)
+                x[m, :, a, c] += dot_nn(coarse, wt[:, at : at + D]).reshape(12, 8, D)
+
+    def embed_all(m):
+        embedded = embed([xs[m, pl.ds(a, 24, stride=4), :] for a in range(4)])
+        x[m] = embedded.reshape(12, 2, 2, 8, D)
+
+    def make_skip(m):
+        whole = (x[m].reshape(FINE, D) + dot_nn(mixed[m], wo[...])).astype(BF16)
+        x[m] = whole.astype(F32).reshape(12, 2, 2, 8, D)
 
     def project_fine(m):
         nrm[0:FINE, :] = normed(x[m].reshape(FINE, D), m)
@@ -356,41 +360,72 @@
 
         run_jobs(fine_jobs(nrm.at[0:FINE], 64, OWN, (0, 1, 2), put))
 
-    def attend(queries, keys, values, mask, count):
-        head = iota((count, G), 1) // 64
-        stacked = jnp.concatenate(
-            [jnp.where(head == h, queries, jnp.zeros_like(queries)) for h in range(4)], axis=0
-        )
-        expo = jnp.exp2(dot_nt(stacked, keys)).astype(BF16)
-        expo = expo * jnp.concatenate([mask] * 4, axis=0)
-        mixed = dot_nn(expo, values)
-        total = dot_nn(expo, ones[0 : keys.shape[0], :])
-        part = [mixed[h * count : (h + 1) * count] for h in range(4)]
-        sums = [total[h * count : (h + 1) * count] for h in range(4)]
-        first = head[:, 0:128] == 0
-        number = jnp.concatenate(
-            [
-                jnp.where(first, part[0][:, 0:128], part[1][:, 0:128]),
-                jnp.where(first, part[2][:, 128:256], part[3][:, 128:256]),
-            ],
-            axis=1,
-        )
-        weight = jnp.concatenate(
-            [jnp.where(first, sums[0], sums[1]), jnp.where(first, sums[2], sums[3])], axis=1
-        )
-        return (number / weight).astype(BF16)
+    def attend(items, lags):
+        held = [{} for _ in items]
+
+        def score(i):
+            queries, keys = items[i][0](), items[i][1]()
+            head = iota(queries.shape, 1) // 64
+            stacked = jnp.concatenate(
+                [jnp.where(head == h, queries, jnp.zeros_like(queries)) for h in range(4)], axis=0
+            )
+            held[i]["score"] = dot_nt(stacked, keys)
+
+        def weigh(i):
+            expo = jnp.exp2(held[i].pop("score")).astype(BF16)
+            held[i]["expo"] = expo * jnp.concatenate([items[i][3]()] * 4, axis=0)
+
+        def gather(i):
+            expo = held[i].pop("expo")
+            held[i]["sum"] = jnp.sum(expo.astype(F32), axis=-1, keepdims=True)
+            held[i]["mixed"] = dot_nn(expo, items[i][2]())
+
+        def place_heads(i):
+            total, value = held[i].pop("sum"), held[i].pop("mixed")
+            count = value.shape[0] // 4
+            part = [value[h * count : (h + 1) * count] for h in range(4)]
+            sums = [total[h * count : (h + 1) * count] for h in range(4)]
+            first = iota((count, 128), 1) < 64
+            number = jnp.concatenate(
+                [
+                    jnp.where(first, part[0][:, 0:128], part[1][:, 0:128]),
+                    jnp.where(first, part[2][:, 128:256], part[3][:, 128:256]),
+                ],
+                axis=1,
+            )
+            weight = jnp.concatenate(
+                [jnp.where(first, sums[0], sums[1]), jnp.where(first, sums[2], sums[3])], axis=1
+            )
+            items[i][4]((number / weight).astype(BF16))
+
+        stages = (score, weigh, gather, place_heads)
+        for step in range(len(items) + lags[-1]):
+            for stage, lag in zip(stages, lags):
+                if 0 <= step - lag < len(items):
+                    stage(step - lag)
 
     def mix_fine(m):
+        items = []
         for t in range(2):
             for g in range(2):
-                mix[128 * t : 128 * t + 128, g * G : (g + 1) * G] = attend(
-                    q_s[2 * m + g, 128 * t : 128 * t + 128, :],
-                    k_s[2 * m + g, 128 * t : 128 * t + 256, :],
-                    v_s[2 * m + g, 128 * t : 128 * t + 256, :],
-                    fmask[t],
-                    128,
+                rows, near, cols = pl.ds(128 * t, 128), pl.ds(128 * t, 256), pl.ds(g * G, G)
+
+                def put(value, rows=rows, cols=cols):
+                    mix[m, rows, cols] = value
+
+                items.append(
+                    (
+                        lambda g=g, rows=rows: q_s[2 * m + g, rows, :],
+                        lambda g=g, near=near: k_s[2 * m + g, near, :],
+                        lambda g=g, near=near: v_s[2 * m + g, near, :],
+                        lambda t=t: fmask[t],
+                        put,
+                    )
                 )
-        update = dot_nn(mix[:, 0:FI], w[3 * FI : 4 * FI, :])
+        attend(items, (0, 1, 1, 2))
+
+    def add_fine(m):
+        update = dot_nn(mix[m], w[3 * FI : 4 * FI, :])
         x[m, 2:10] += update.reshape(8, 2, 2, 8, D)
 
     def coarse_jobs(first, count, parts):
@@ -412,24 +447,44 @@
         run_jobs(coarse_jobs(32, COWN, (0,)))
 
     def coarse_rest(m):
-        nrm[0:32, :] = normed(cin[m, 0:32, :].astype(F32), m)
-        nrm[96:128, :] = normed(cin[m, 96:128, :].astype(F32), m)
+        for i in range(2):
+            edge = edge_in[m, i].astype(F32)
+            edge = jnp.concatenate([edge[0:24], edge[24:48]], axis=1)
+            at = (8, 96)[i]
+            nrm[at : at + 24, :] = normed(edge, m)
         run_jobs(coarse_jobs(0, COARSE, (1, 2)))
+        items = []
         for g in range(6):
-            mix[0:COWN, g * G : (g + 1) * G] = attend(
-                q_s[g, 0:COWN, :], k_s[g, 0:COARSE, :], v_s[g, 0:COARSE, :], cmask[...], COWN
+
+            def put(value, g=g):
+                grp[:, g * G : (g + 1) * G] = value
+
+            items.append(
+                (
+                    lambda g=g: q_s[g, 0:COWN, :],
+                    lambda g=g: k_s[g, 0:COARSE, :],
+                    lambda g=g: v_s[g, 0:COARSE, :],
+                    lambda: cmask[...],
+                    put,
+                )
             )
-        update = dot_nn(mix[0:COWN, :], w[3 * CI : 4 * CI, :])
-        cout[m] = (cin[m, 32:96, :].astype(F32) + update).astype(BF16)
+        attend(items, (0, 1, 2, 3))
+        update = dot_nn(grp[:, 0:CI], w[3 * CI : 4 * CI, :])
+        put_coarse(m, cin[m, 32:96, :].astype(F32) + update)
+
+    def put_coarse(m, result):
+        cout[m] = result.astype(BF16)
+        for i in range(2):
+            rows = result[0:24] if i == 0 else result[40:64]
+            edge_out[m, i] = jnp.concatenate([rows[:, 0:512], rows[:, 512:1024]], axis=0).astype(BF16)
 
     def merge(m):
         own = x[m, 2:10]
-        skip[m, 64:320, :] = own.reshape(OWN, D).astype(BF16)
         for a in range(2):
             for c in range(2):
                 at = (2 * a + c) * D
                 grp[:, at : at + D] = own[:, a, c].reshape(COWN, D).astype(BF16)
-        cout[m] = dot_nn(grp[...], w[4 * FI :, :]).astype(BF16)
+        put_coarse(m, dot_nn(grp[...], w[4 * FI :, :]))
 
     def head(m):
         top = x[m, 2:10].reshape(OWN, D)
@@ -446,63 +501,70 @@
     def coarse_own(m, seg):
         return remote(cout.at[m], cin.at[m, pl.ds(32, 64), :], c_s.at[m, 0], c_r.at[m, 0], seg + 1, b)
 
-    def coarse_up(m, seg, rows):
-        return remote(
-            cout.at[m, pl.ds(0, rows), :], cin.at[m, pl.ds(96, rows), :], c_s.at[m, 1], c_r.at[m, 2], seg + 1, b - 1
-        )
-
-    def coarse_down(m, seg, rows):
-        return remote(
-            cout.at[m, pl.ds(64 - rows, rows), :], cin.at[m, pl.ds(32 - rows, rows), :],
-            c_s.at[m, 2], c_r.at[m, 1], seg + 1, b + 1,
-        )
-
-    def send_coarse(m, seg, rows, act):
+    def edge_up(m, seg):
+        if seg < 2:
+            src, dst = edge_out.at[m, 0], edge_in.at[m, 1]
+        else:
+            src, dst = cout.at[m, pl.ds(0, 16), :], cin.at[m, pl.ds(96, 16), :]
+        return remote(src, dst, c_s.at[m, 1], c_r.at[m, 2], seg + 1, b - 1)
+
+    def edge_down(m, seg):
+        if seg < 2:
+            src, dst = edge_out.at[m, 1], edge_in.at[m, 0]
+        else:
+            src, dst = cout.at[m, pl.ds(48, 16), :], cin.at[m, pl.ds(16, 16), :]
+        return remote(src, dst, c_s.at[m, 2], c_r.at[m, 1], seg + 1, b + 1)
+
+    def send_coarse(m, seg, act):
         @pl.when(has_up)
         def _():
-            act(coarse_up(m, seg, rows))
+            act(edge_up(m, seg))
 
         @pl.when(has_down)
         def _():
-            act(coarse_down(m, seg, rows))
+            act(edge_down(m, seg))
 
         act(coarse_own(m, seg))
 
     def take_own(m):
         arrived(cin.at[m, pl.ds(32, 64), :], c_r.at[m, 0])
 
-    def take_halos(m, rows):
+    def take_edges(m, above, below):
         @pl.when(has_up)
         def _():
-            arrived(cin.at[m, pl.ds(32 - rows, rows), :], c_r.at[m, 1])
+            arrived(above, c_r.at[m, 1])
 
         @pl.when(has_down)
         def _():
-            arrived(cin.at[m, pl.ds(96, rows), :], c_r.at[m, 2])
-
-    def skip_copy(m):
+            arrived(below, c_r.at[m, 2])
+
+    def pixels_on():
+        return remote(xs, xs, xs_s, xs_r, 3, b)
+
+    def weights_on():
+        return remote(w_hbm.at[0, pl.ds(3 * FI, FI), :], wo, wo_s, wo_r, 3, b)
+
+    def mix_copy(m):
+        return remote(mix.at[m], mixed.at[m, pl.ds(64, OWN), :], mix_s.at[m], mix_r.at[m], 3, b)
+
+    def mix_up(m):
         return remote(
-            skip.at[m, pl.ds(64, OWN), :], skip.at[m, pl.ds(64, OWN), :], skip_s.at[m], skip_r.at[m], 3, b
+            mixed.at[m, pl.ds(64, 64), :], mixed.at[m, pl.ds(320, 64), :], fwd_s.at[m, 0], fwd_r.at[m, 1], 3, b - 1
         )
 
-    def skip_up(m):
+    def mix_down(m):
         return remote(
-            skip.at[m, pl.ds(64, 64), :], skip.at[m, pl.ds(320, 64), :], fwd_s.at[m, 0], fwd_r.at[m, 1], 3, b - 1
+            mixed.at[m, pl.ds(256, 64), :], mixed.at[m, pl.ds(0, 64), :], fwd_s.at[m, 1], fwd_r.at[m, 0], 3, b + 1
         )
 
-    def skip_down(m):
-        return remote(
-            skip.at[m, pl.ds(256, 64), :], skip.at[m, pl.ds(0, 64), :], fwd_s.at[m, 1], fwd_r.at[m, 0], 3, b + 1
-        )
-
-    def forward_skip(m, act):
+    def forward_mix(m, act):
         @pl.when(has_up)
         def _():
-            act(skip_up(m))
+            act(mix_up(m))
 
         @pl.when(has_down)
         def _():
-            act(skip_down(m))
+            act(mix_down(m))
 
     def pixel_copy(m, seg):
         return pltpu.make_async_remote_copy(
@@ -516,56 +578,53 @@
     def sent(copy):
         copy.wait_send()
 
+    @pl.when(s == 0)
+    def _():
+        frame_copy.wait()
+        noise_copy.wait()
+        scale_pixels()
+        pl.semaphore_wait(barrier, 2 + 2 * edges)
+
+        @pl.when(has_up)
+        def _():
+            halo_up().start()
+
+        @pl.when(has_down)
+        def _():
+            halo_down().start()
+
+        weights_on().start()
+
     freq_copy.wait()
     cond_copy.wait()
     make_gains()
 
-    @pl.when(s == 0)
-    def _():
-        frame_copy.wait()
-        noise_copy.wait()
-        scale_pixels()
+    @pl.when((s == 0) | (s == 3))
+    def _():
         patch_in_copy.wait()
         make_embedding()
+
+    @pl.when(s == 0)
+    def _():
         make_fine_links()
         make_fine_mask()
-        embed_own()
-        pl.semaphore_wait(barrier, 2 + 2 * edges)
-
-        @pl.when(has_up)
-        def _():
-            halo_up().start()
-
-        @pl.when(has_down)
-        def _():
-            halo_down().start()
-
         link_copy(3).start()
+        embed_own(0)
         for i in range(3 * FI // CHUNK):
             weight_copy(i).wait()
-        project_own()
-
-        @pl.when(has_up)
-        def _():
-            arrived(xs.at[:, pl.ds(0, 16), :], halo_r.at[0])
-
-        @pl.when(has_down)
-        def _():
-            arrived(xs.at[:, pl.ds(80, 16), :], halo_r.at[1])
-
-        project_halo()
-        for i in range(3 * FI // CHUNK, CHUNKS):
-            weight_copy(i).wait()
 
     @pl.when((s == 1) | (s == 2))
     def _():
+        nrm[0:8, :] = jnp.zeros((8, D), BF16)
+        nrm[120:128, :] = jnp.zeros((8, D), BF16)
+
         @pl.when(b == 0)
         def _():
-            cin[:, 0:32, :] = jnp.zeros((MB, 32, D), BF16)
+            edge_in[:, 0] = jnp.zeros((MB, 48, 512), BF16)
 
         @pl.when(b == n_space - 1)
         def _():
-            cin[:, 96:128, :] = jnp.zeros((MB, 32, D), BF16)
+            edge_in[:, 1] = jnp.zeros((MB, 48, 512), BF16)
 
         transpose_weights(0, 3 * CI // G)
         for i in range(3 * CI // CHUNK, CHUNKS):
@@ -588,12 +647,12 @@
         @pl.when(b == 0)
         def _():
             cin[:, 16:32, :] = jnp.zeros((MB, 16, D), BF16)
-            skip[:, 0:64, :] = jnp.zeros((MB, 64, D), BF16)
+            mixed[:, 0:64, :] = jnp.zeros((MB, 64, FI), BF16)
 
         @pl.when(b == n_space - 1)
         def _():
             cin[:, 96:112, :] = jnp.zeros((MB, 16, D), BF16)
-            skip[:, 320:384, :] = jnp.zeros((MB, 64, D), BF16)
+            mixed[:, 320:384, :] = jnp.zeros((MB, 64, FI), BF16)
 
         for i in range(4 * FI // CHUNK):
             weight_copy(i).wait()
@@ -608,41 +667,69 @@
         pl.semaphore_wait(barrier, 4 + edges)
         arrived(links, link_r)
         make_fine_mask()
-        arrived(skip.at[0, pl.ds(64, OWN), :], skip_r.at[0])
-        forward_skip(0, start)
-
-    def one_batch(m, carry):
-        @pl.when(s == 3)
-        def _():
-            take_own(m)
-            take_halos(m, 16)
+        arrived(xs, xs_r)
+        for m in range(MB):
+            embed_all(m)
+        arrived(wo, wo_r)
+        for m in range(MB):
+            arrived(mixed.at[m, pl.ds(64, OWN), :], mix_r.at[m])
+            forward_mix(m, start)
+        for m in range(MB):
 
             @pl.when(has_up)
             def _():
-                arrived(skip.at[m, pl.ds(0, 64), :], fwd_r.at[m, 0])
+                arrived(mixed.at[m, pl.ds(0, 64), :], fwd_r.at[m, 0])
 
             @pl.when(has_down)
             def _():
-                arrived(skip.at[m, pl.ds(320, 64), :], fwd_r.at[m, 1])
-
-            widen(m)
+                arrived(mixed.at[m, pl.ds(320, 64), :], fwd_r.at[m, 1])
+
+            make_skip(m)
+
+    def one_batch(m, carry):
+        @pl.when(s == 0)
+        def _():
+            project_own(m)
 
             @pl.when(m == 0)
             def _():
-                arrived(skip.at[1, pl.ds(64, OWN), :], skip_r.at[1])
-                forward_skip(1, start)
-
+                embed_own(1)
+
+                @pl.when(has_up)
+                def _():
+                    arrived(xs.at[:, pl.ds(0, 16), :], halo_r.at[0])
+
+                @pl.when(has_down)
+                def _():
+                    arrived(xs.at[:, pl.ds(80, 16), :], halo_r.at[1])
+
+                pixels_on().start()
+                for i in range(3 * FI // CHUNK, CHUNKS):
+                    weight_copy(i).wait()
+
+            project_halo(m)
+
+        @pl.when(s == 3)
+        def _():
+            take_own(m)
+            take_edges(m, cin.at[m, pl.ds(16, 16), :], cin.at[m, pl.ds(96, 16), :])
+            widen(m)
             project_fine(m)
 
         @pl.when((s == 0) | (s == 3))
         def _():
             mix_fine(m)
 
+            @pl.when(s == 0)
+            def _():
+                mix_copy(m).start()
+
+            add_fine(m)
+
         @pl.when(s == 0)
         def _():
             merge(m)
-            send_coarse(m, 0, 32, start)
-            skip_copy(m).start()
+            send_coarse(m, 0, start)
 
         @pl.when(s == 3)
         def _():
@@ -654,16 +741,16 @@
         def _():
             take_own(m)
             coarse_queries(m)
-            take_halos(m, 32)
+            take_edges(m, edge_in.at[m, 0], edge_in.at[m, 1])
             coarse_rest(m)
 
         @pl.when(s == 1)
         def _():
-            send_coarse(m, 1, 32, start)
+            send_coarse(m, 1, start)
 
         @pl.when(s == 2)
         def _():
-            send_coarse(m, 2, 16, start)
+            send_coarse(m, 2, start)
 
         return carry
 
@@ -689,24 +776,26 @@
 
         link_copy(3).wait_send()
         for m in range(MB):
-            send_coarse(m, 0, 32, sent)
-            skip_copy(m).wait_send()
+            send_coarse(m, 0, sent)
+            mix_copy(m).wait_send()
+        weights_on().wait_send()
+        pixels_on().wait_send()
 
     @pl.when(s == 1)
     def _():
         link_copy(2).wait_send()
         for m in range(MB):
-            send_coarse(m, 1, 32, sent)
+            send_coarse(m, 1, sent)
 
     @pl.when(s == 2)
     def _():
         for m in range(MB):
-            send_coarse(m, 2, 16, sent)
+            send_coarse(m, 2, sent)
 
     @pl.when(s == 3)
     def _():
         for m in range(MB):
-            forward_skip(m, sent)
+            forward_mix(m, sent)
             for seg in range(4):
                 pixel_copy(m, seg).wait_send()
 
@@ -736,15 +825,18 @@
             pltpu.VMEM((MB, 96, 128), F32),
             pltpu.VMEM((MB, 12, 2, 2, 8, D), F32),
             pltpu.VMEM((2 * OWN, D), BF16),
-            pltpu.VMEM((256, D), BF16),
+            pltpu.VMEM((128, D), BF16),
             pltpu.VMEM((6, OWN, G), BF16),
             pltpu.VMEM((6, FINE, G), BF16),
             pltpu.VMEM((6, FINE, G), BF16),
-            pltpu.VMEM((OWN, CI), BF16),
+            pltpu.VMEM((MB, OWN, FI), BF16),
+            pltpu.VMEM((MB, FINE, FI), BF16),
             pltpu.VMEM((COWN, 4 * D), BF16),
-            pltpu.VMEM((MB, FINE, D), BF16),
+            pltpu.VMEM((FI, D), BF16),
             pltpu.VMEM((MB, COARSE, D), BF16),
             pltpu.VMEM((MB, COWN, D), BF16),
+            pltpu.VMEM((MB, 2, 48, 512), BF16),
+            pltpu.VMEM((MB, 2, 48, 512), BF16),
             pltpu.VMEM((768, D), BF16),
             pltpu.VMEM((D, 256), BF16),
             pltpu.VMEM((8, D), F32),
@@ -760,6 +852,8 @@
             dma((2,)), dma((2,)),
             dma(()), dma(()),
             dma((MB, 3)), dma((MB, 3)),
+            dma(()), dma(()),
+            dma(()), dma(()),
             dma((MB,)), dma((MB,)),
             dma((MB, 2)), dma((MB, 2)),
             dma((MB, 4)), dma((MB,)),

time: 58.5 us -> 52.1 us (0.89)
  the two profiles are of different devices: /device:TPU:129 before, /device:TPU:161 now
where the time goes in v3:
time: 52.1 us; the launch traced here: 51.9 us
  Pallas kernels  50.6 us (97%)
  local copies, waits for them, and re-layouts  1.32 us (3%)
    pallas_call x1, Pallas kernels, per_device(): pl.pallas_call(functools.partial(kernel, lax.axis_size('space')), out_sha...  50.6 us
    unnamed x1, local copies, waits for them, and re-layouts  1.32 us

profile of v3, /device:TPU:161, one launch (start us, length us, event | category | flops | bytes accessed | tf_op | source)
XLA Modules:
  0.0 51.9 jit_solution(8347764810544440022)
XLA Ops:
  0.0 50.6 %shard_map.109 = f32[2,16,64]{2,1,0:T(8,128)} custom-call(f32[2,64,64]{2,1,0:T(8,128)} %frames_hbm.1, f32[2,64,64]{2,1,0:T(8,128)} %noise_hbm.1, s32[2]{0:T(128)} %steps.1, f32[128]{0:T(128)} %freqs_hbm.1, bf16[1,256,1024]{2,1,0:T(8,128)(2,1)} %cond_hbm.1, f32[16,1024]{1,0:T(8,128)} %patch_in_hbm.1, bf16[16,1024]{1,0:T(8,128)(2,1)} %bitcast.3, ...), custom_call_target="tpu_custom_call" | custom-call | tf_op jit(solution)/shard_map/pallas_call | solution.py:811
  50.6 1.3 %copy.13 = f32[2,64,16]{1,2,0:T(8,128)} copy(f32[2,64,16]{1,2,0:T(8,128)} %bitcast.2) | data formatting | bytes 16384

commit v4 on v3

--- a/solution.py
+++ b/solution.py
@@ -29,8 +29,8 @@
 NT = (((1,), (1,)), ((), ()))
 NN = (((1,), (0,)), ((), ()))
 
-CHUNK = 256
-CHUNKS = 24
+CHUNK = 1536
+CHUNKS = 4
 
 
 def dot_nt(a, b):
@@ -59,7 +59,7 @@
     out,
     w, wt, frames, noise, freqs, cond, patch_in, patch_out, xs, x, nrm, halo, q_s, k_s, v_s, mix, mixed, grp, wo, cin, cout,
     edge_out, edge_in, w3, pox, gains, qscale, links, fmask, cmask, pixout, pixin, placed,
-    w_sem, in_sem, halo_s, halo_r, link_s, link_r, c_s, c_r, xs_s, xs_r, wo_s, wo_r, mix_s, mix_r, fwd_s,
+    w_sem, in_sem, halo_s, halo_r, link_s, link_r, c_s, c_r, xs_s, xs_r, wo_s, wo_r, wx_s, wx_r, mix_s, mix_r, fwd_s,
     fwd_r, pix_s, pix_r,
 ):
     s = lax.axis_index("segment")
@@ -120,8 +120,12 @@
 
     freq_copy.start()
     cond_copy.start()
-    for i in range(CHUNKS):
-        weight_copy(i).start()
+    weight_copy(0).start()
+
+    @pl.when(s > 0)
+    def _():
+        for i in range(1, CHUNKS):
+            weight_copy(i).start()
 
     greet(3, place(3, p))
 
@@ -140,6 +144,7 @@
     @pl.when(s == 3)
     def _():
         greet(0, b)
+        greet(1, b)
         patch_out_copy.start()
 
     def level_row(m):
@@ -242,19 +247,18 @@
         w3[256:512, :] = dot_nn(pick, low).astype(BF16)
         w3[512:768, :] = wide
 
-    def transpose_weights(first, count):
+    def transpose_weights(first, last, base):
         eye = (iota((G, G), 0) == iota((G, G), 1)).astype(BF16)
 
         def tile(i, carry):
-            weight_copy(first + i).wait()
-            row = pl.multiple_of((first + i) * G, G)
-            col = pl.multiple_of(i * G, G)
+            row = pl.multiple_of(i * G, G)
+            col = pl.multiple_of((i - base) * G, G)
             for k in range(D // G):
                 block = dot_nt(eye, w[pl.ds(row, G), k * G : (k + 1) * G])
                 wt[k * G : (k + 1) * G, pl.ds(col, G)] = block.astype(BF16)
             return carry
 
-        lax.fori_loop(0, count, tile, 0)
+        lax.fori_loop(first, last, tile, 0)
 
     def normed(value, m):
         scale = lax.rsqrt(jnp.mean(value * value, axis=-1, keepdims=True) + EPS)
@@ -516,6 +520,8 @@
         return remote(src, dst, c_s.at[m, 2], c_r.at[m, 1], seg + 1, b + 1)
 
     def send_coarse(m, seg, act):
+        act(coarse_own(m, seg))
+
         @pl.when(has_up)
         def _():
             act(edge_up(m, seg))
@@ -523,8 +529,6 @@
         @pl.when(has_down)
         def _():
             act(edge_down(m, seg))
-
-        act(coarse_own(m, seg))
 
     def take_own(m):
         arrived(cin.at[m, pl.ds(32, 64), :], c_r.at[m, 0])
@@ -541,8 +545,20 @@
     def pixels_on():
         return remote(xs, xs, xs_s, xs_r, 3, b)
 
-    def weights_on():
-        return remote(w_hbm.at[0, pl.ds(3 * FI, FI), :], wo, wo_s, wo_r, 3, b)
+    def half(which):
+        return wo.at[pl.ds(pl.multiple_of(which * 256, 256), 256), :]
+
+    mine, other = b % 2, 1 - b % 2
+
+    def half_copy():
+        rows = pl.ds(pl.multiple_of(3 * FI + mine * 256, 256), 256)
+        return pltpu.make_async_copy(w_hbm.at[0, rows, :], half(mine), in_sem.at[6])
+
+    def weights_on(seg):
+        return remote(half(mine), half(mine), wo_s, wo_r, seg, b)
+
+    def weights_across():
+        return remote(half(mine), half(mine), wx_s, wx_r, 3, b + 1 - 2 * mine)
 
     def mix_copy(m):
         return remote(mix.at[m], mixed.at[m, pl.ds(64, OWN), :], mix_s.at[m], mix_r.at[m], 3, b)
@@ -578,6 +594,11 @@
     def sent(copy):
         copy.wait_send()
 
+    def take_gains():
+        freq_copy.wait()
+        cond_copy.wait()
+        make_gains()
+
     @pl.when(s == 0)
     def _():
         frame_copy.wait()
@@ -593,25 +614,43 @@
         def _():
             halo_down().start()
 
-        weights_on().start()
-
-    freq_copy.wait()
-    cond_copy.wait()
-    make_gains()
-
-    @pl.when((s == 0) | (s == 3))
-    def _():
+        half_copy().start()
+        make_fine_links()
+        link_copy(3).start()
+        take_gains()
         patch_in_copy.wait()
         make_embedding()
-
-    @pl.when(s == 0)
-    def _():
-        make_fine_links()
+        embed_own(0)
+        half_copy().wait()
+        weights_on(1).start()
+        weight_copy(0).wait()
+        for i in range(1, CHUNKS):
+            weight_copy(i).start()
+        project_own(0)
         make_fine_mask()
-        link_copy(3).start()
-        embed_own(0)
-        for i in range(3 * FI // CHUNK):
-            weight_copy(i).wait()
+
+        @pl.when(has_up)
+        def _():
+            arrived(xs.at[:, pl.ds(0, 16), :], halo_r.at[0])
+
+        @pl.when(has_down)
+        def _():
+            arrived(xs.at[:, pl.ds(80, 16), :], halo_r.at[1])
+
+        pixels_on().start()
+        for m in range(MB):
+            if m > 0:
+                embed_own(m)
+                project_own(m)
+            project_halo(m)
+            mix_fine(m)
+            if m == 0:
+                for i in range(1, CHUNKS):
+                    weight_copy(i).wait()
+            add_fine(m)
+            merge(m)
+            send_coarse(m, 0, start)
+            mix_copy(m).start()
 
     @pl.when((s == 1) | (s == 2))
     def _():
@@ -626,21 +665,43 @@
         def _():
             edge_in[:, 1] = jnp.zeros((MB, 48, 512), BF16)
 
-        transpose_weights(0, 3 * CI // G)
-        for i in range(3 * CI // CHUNK, CHUNKS):
+        @pl.when(s == 1)
+        def _():
+            make_coarse_links()
+            pl.semaphore_wait(barrier, 2 + edges)
+            link_copy(2).start()
+            arrived(half(mine), wo_r)
+            weights_on(3).start()
+
+        @pl.when(s == 2)
+        def _():
+            pl.semaphore_wait(barrier, 1 + edges)
+            arrived(links, link_r)
+
+        make_coarse_mask()
+        take_gains()
+        for i in range(3):
             weight_copy(i).wait()
-        pl.semaphore_wait(barrier, 1 + edges)
-
-    @pl.when(s == 1)
-    def _():
-        make_coarse_links()
-        link_copy(2).start()
-        make_coarse_mask()
-
-    @pl.when(s == 2)
-    def _():
-        arrived(links, link_r)
-        make_coarse_mask()
+            transpose_weights(6 * i, 6 * i + 6, 0)
+        weight_copy(3).wait()
+
+        def one_batch(m, carry):
+            take_own(m)
+            coarse_queries(m)
+            take_edges(m, edge_in.at[m, 0], edge_in.at[m, 1])
+            coarse_rest(m)
+
+            @pl.when(s == 1)
+            def _():
+                send_coarse(m, 1, start)
+
+            @pl.when(s == 2)
+            def _():
+                send_coarse(m, 2, start)
+
+            return carry
+
+        lax.fori_loop(0, MB, one_batch, 0)
 
     @pl.when(s == 3)
     def _():
@@ -654,9 +715,9 @@
             cin[:, 96:112, :] = jnp.zeros((MB, 16, D), BF16)
             mixed[:, 320:384, :] = jnp.zeros((MB, 64, FI), BF16)
 
-        for i in range(4 * FI // CHUNK):
-            weight_copy(i).wait()
-        transpose_weights(4 * FI // G, 4 * D // G)
+        take_gains()
+        patch_in_copy.wait()
+        make_embedding()
         patch_out_copy.wait()
         entry = iota((16, 256), 0)
         col = iota((16, 256), 1)
@@ -664,13 +725,22 @@
         pox[...] = lax.dot_general(
             patch_out[...], pick, (((0,), (0,)), ((), ())), preferred_element_type=F32
         ).astype(BF16)
+        weight_copy(0).wait()
+        weight_copy(1).wait()
+        transpose_weights(8, 12, 8)
+        weight_copy(2).wait()
+        transpose_weights(12, 18, 8)
+        weight_copy(3).wait()
+        transpose_weights(18, 24, 8)
         pl.semaphore_wait(barrier, 4 + edges)
         arrived(links, link_r)
         make_fine_mask()
+        arrived(half(mine), wo_r)
+        weights_across().start()
         arrived(xs, xs_r)
         for m in range(MB):
             embed_all(m)
-        arrived(wo, wo_r)
+        arrived(half(other), wx_r)
         for m in range(MB):
             arrived(mixed.at[m, pl.ds(64, OWN), :], mix_r.at[m])
             forward_mix(m, start)
@@ -686,75 +756,19 @@
 
             make_skip(m)
 
-    def one_batch(m, carry):
-        @pl.when(s == 0)
-        def _():
-            project_own(m)
-
-            @pl.when(m == 0)
-            def _():
-                embed_own(1)
-
-                @pl.when(has_up)
-                def _():
-                    arrived(xs.at[:, pl.ds(0, 16), :], halo_r.at[0])
-
-                @pl.when(has_down)
-                def _():
-                    arrived(xs.at[:, pl.ds(80, 16), :], halo_r.at[1])
-
-                pixels_on().start()
-                for i in range(3 * FI // CHUNK, CHUNKS):
-                    weight_copy(i).wait()
-
-            project_halo(m)
-
-        @pl.when(s == 3)
-        def _():
+        def one_batch(m, carry):
             take_own(m)
             take_edges(m, cin.at[m, pl.ds(16, 16), :], cin.at[m, pl.ds(96, 16), :])
             widen(m)
             project_fine(m)
-
-        @pl.when((s == 0) | (s == 3))
-        def _():
             mix_fine(m)
-
-            @pl.when(s == 0)
-            def _():
-                mix_copy(m).start()
-
             add_fine(m)
-
-        @pl.when(s == 0)
-        def _():
-            merge(m)
-            send_coarse(m, 0, start)
-
-        @pl.when(s == 3)
-        def _():
             head(m)
             for seg in range(4):
                 pixel_copy(m, seg).start()
-
-        @pl.when((s == 1) | (s == 2))
-        def _():
-            take_own(m)
-            coarse_queries(m)
-            take_edges(m, edge_in.at[m, 0], edge_in.at[m, 1])
-            coarse_rest(m)
-
-        @pl.when(s == 1)
-        def _():
-            send_coarse(m, 1, start)
-
-        @pl.when(s == 2)
-        def _():
-            send_coarse(m, 2, start)
-
-        return carry
-
-    lax.fori_loop(0, MB, one_batch, 0)
+            return carry
+
+        lax.fori_loop(0, MB, one_batch, 0)
 
     for m in range(MB):
         arrived(pixin.at[m], pix_r.at[m])
@@ -778,12 +792,13 @@
         for m in range(MB):
             send_coarse(m, 0, sent)
             mix_copy(m).wait_send()
-        weights_on().wait_send()
+        weights_on(1).wait_send()
         pixels_on().wait_send()
 
     @pl.when(s == 1)
     def _():
         link_copy(2).wait_send()
+        weights_on(3).wait_send()
         for m in range(MB):
             send_coarse(m, 1, sent)
 
@@ -794,6 +809,7 @@
 
     @pl.when(s == 3)
     def _():
+        weights_across().wait_send()
         for m in range(MB):
             forward_mix(m, sent)
             for seg in range(4):
@@ -848,10 +864,11 @@
             pltpu.VMEM((MB, 16, 128), F32),
             pltpu.VMEM((64, 128), F32),
             dma((CHUNKS,)),
-            dma((6,)),
+            dma((7,)),
             dma((2,)), dma((2,)),
             dma(()), dma(()),
             dma((MB, 3)), dma((MB, 3)),
+            dma(()), dma(()),
             dma(()), dma(()),
             dma(()), dma(()),
             dma((MB,)), dma((MB,)),

time: 52.1 us -> 47.4 us (0.910)
  the two profiles are of different devices: /device:TPU:161 before, /device:TPU:129 now
where the time goes in v4:
time: 47.4 us; the launch traced here: 47.1 us
  Pallas kernels  45.8 us (97%)
  local copies, waits for them, and re-layouts  1.32 us (3%)
    pallas_call x1, Pallas kernels, per_device(): pl.pallas_call(functools.partial(kernel, lax.axis_size('space')), out_sha...  45.8 us
    unnamed x1, local copies, waits for them, and re-layouts  1.32 us

profile of v4, /device:TPU:129, one launch (start us, length us, event | category | flops | bytes accessed | tf_op | source)
XLA Modules:
  0.0 47.1 jit_solution(14141979653232553257)
XLA Ops:
  0.0 45.8 %shard_map.109 = f32[2,16,64]{2,1,0:T(8,128)} custom-call(f32[2,64,64]{2,1,0:T(8,128)} %frames_hbm.1, f32[2,64,64]{2,1,0:T(8,128)} %noise_hbm.1, s32[2]{0:T(128)} %steps.1, f32[128]{0:T(128)} %freqs_hbm.1, bf16[1,256,1024]{2,1,0:T(8,128)(2,1)} %cond_hbm.1, f32[16,1024]{1,0:T(8,128)} %patch_in_hbm.1, bf16[16,1024]{1,0:T(8,128)(2,1)} %bitcast.3, ...), custom_call_target="tpu_custom_call" | custom-call | tf_op jit(solution)/shard_map/pallas_call | solution.py:827
  45.8 1.3 %copy.13 = f32[2,64,16]{1,2,0:T(8,128)} copy(f32[2,64,16]{1,2,0:T(8,128)} %bitcast.2) | data formatting | bytes 16384

commit v5 on v4

--- a/solution.py
+++ b/solution.py
@@ -744,8 +744,8 @@
         for m in range(MB):
             arrived(mixed.at[m, pl.ds(64, OWN), :], mix_r.at[m])
             forward_mix(m, start)
-        for m in range(MB):
-
+
+        def one_batch(m, carry):
             @pl.when(has_up)
             def _():
                 arrived(mixed.at[m, pl.ds(0, 64), :], fwd_r.at[m, 0])
@@ -755,8 +755,6 @@
                 arrived(mixed.at[m, pl.ds(320, 64), :], fwd_r.at[m, 1])
 
             make_skip(m)
-
-        def one_batch(m, carry):
             take_own(m)
             take_edges(m, cin.at[m, pl.ds(16, 16), :], cin.at[m, pl.ds(96, 16), :])
             widen(m)

time: 47.4 us -> 47.5 us (level)
  no operation moved by 1% of the time
where the time goes in v5:
time: 47.5 us; the launch traced here: 47.3 us
  Pallas kernels  45.9 us (97%)
  local copies, waits for them, and re-layouts  1.32 us (3%)
    pallas_call x1, Pallas kernels, per_device(): pl.pallas_call(functools.partial(kernel, lax.axis_size('space')), out_sha...  45.9 us
    unnamed x1, local copies, waits for them, and re-layouts  1.32 us

profile of v5, /device:TPU:129, one launch (start us, length us, event | category | flops | bytes accessed | tf_op | source)
XLA Modules:
  0.0 47.3 jit_solution(12974618044167857399)
XLA Ops:
  0.0 45.9 %shard_map.109 = f32[2,16,64]{2,1,0:T(8,128)} custom-call(f32[2,64,64]{2,1,0:T(8,128)} %frames_hbm.1, f32[2,64,64]{2,1,0:T(8,128)} %noise_hbm.1, s32[2]{0:T(128)} %steps.1, f32[128]{0:T(128)} %freqs_hbm.1, bf16[1,256,1024]{2,1,0:T(8,128)(2,1)} %cond_hbm.1, f32[16,1024]{1,0:T(8,128)} %patch_in_hbm.1, bf16[16,1024]{1,0:T(8,128)(2,1)} %bitcast.3, ...), custom_call_target="tpu_custom_call" | custom-call | tf_op jit(solution)/shard_map/pallas_call | solution.py:825
  45.9 1.3 %copy.13 = f32[2,64,16]{1,2,0:T(8,128)} copy(f32[2,64,16]{1,2,0:T(8,128)} %bitcast.2) | data formatting | bytes 16384

commit v6 on v4

--- a/solution.py
+++ b/solution.py
@@ -520,7 +520,8 @@
         return remote(src, dst, c_s.at[m, 2], c_r.at[m, 1], seg + 1, b + 1)
 
     def send_coarse(m, seg, act):
-        act(coarse_own(m, seg))
+        if seg < 2:
+            act(coarse_own(m, seg))
 
         @pl.when(has_up)
         def _():
@@ -529,6 +530,9 @@
         @pl.when(has_down)
         def _():
             act(edge_down(m, seg))
+
+        if seg == 2:
+            act(coarse_own(m, seg))
 
     def take_own(m):
         arrived(cin.at[m, pl.ds(32, 64), :], c_r.at[m, 0])

time: 47.4 us -> 47.4 us (level)
  no operation moved by 1% of the time
where the time goes in v6:
time: 47.4 us; the launch traced here: 47.1 us
  Pallas kernels  45.8 us (97%)
  local copies, waits for them, and re-layouts  1.32 us (3%)
    pallas_call x1, Pallas kernels, per_device(): pl.pallas_call(functools.partial(kernel, lax.axis_size('space')), out_sha...  45.8 us
    unnamed x1, local copies, waits for them, and re-layouts  1.32 us

profile of v6, /device:TPU:129, one launch (start us, length us, event | category | flops | bytes accessed | tf_op | source)
XLA Modules:
  0.0 47.1 jit_solution(11086296134799739446)
XLA Ops:
  0.0 45.8 %shard_map.109 = f32[2,16,64]{2,1,0:T(8,128)} custom-call(f32[2,64,64]{2,1,0:T(8,128)} %frames_hbm.1, f32[2,64,64]{2,1,0:T(8,128)} %noise_hbm.1, s32[2]{0:T(128)} %steps.1, f32[128]{0:T(128)} %freqs_hbm.1, bf16[1,256,1024]{2,1,0:T(8,128)(2,1)} %cond_hbm.1, f32[16,1024]{1,0:T(8,128)} %patch_in_hbm.1, bf16[16,1024]{1,0:T(8,128)(2,1)} %bitcast.3, ...), custom_call_target="tpu_custom_call" | custom-call | tf_op jit(solution)/shard_map/pallas_call | solution.py:831
  45.8 1.3 %copy.13 = f32[2,64,16]{1,2,0:T(8,128)} copy(f32[2,64,16]{1,2,0:T(8,128)} %bitcast.2) | data formatting | bytes 16384
